TPU v7x, 32 devices: a whole 2x2x4 slice. The times are simulated.
32 devices in a mesh: fsdp: 16 (over z, y, x), dp: 2 (over core).
Axes of the slice: x: 2, y: 2, z: 4, core: 2. Of those that a mesh axis runs over, the one named last changes fastest.
Arguments:
- kmer_identifiers: int32 [32, 512], P(('fsdp', 'dp')), may hold values from 0 to 4100
- slot_fragment_ids: int32 [32, 512], P(('fsdp', 'dp')), may hold values from 0 to 32, never falling along the last dimension, each value on 1 to 32 neighbouring positions
- mirror_fragment_index: int32 [1024], P(('fsdp', 'dp')), may hold values from 0 to 1023, as said below
- fragment_weight: float32 [1024], P(('fsdp', 'dp')), may hold values from 0.15 to 4.8, as said below
- affinity_heat: float32 [], replicated, may hold values from 0.05 to 0.1
- optimizer_iteration: int32 [], replicated, may hold values from 2 to 20
- lexicon_table: float32 [4101, 768], P(None, 'fsdp'), may hold values from -6 to 6
- lexicon_first_moment: float32 [4101, 768], P(None, 'fsdp'), may hold values from -2.2351742e-08 to 2.2351742e-08
- lexicon_raw_moment: float32 [4101, 768], P(None, 'fsdp'), may hold values from 9.784441e-19 to 3.9137765e-18
- query_key_value_maps: float32 [768, 2304], P('fsdp'), may hold values from -0.21875 to 0.21875
- qkv_first_moment: float32 [768, 2304], P('fsdp'), may hold values from -2.0861626e-07 to 2.0861626e-07
- qkv_raw_moment: float32 [768, 2304], P('fsdp'), may hold values from 9.7844415e-17 to 3.9137766e-16
- attention_exit_map: float32 [768, 768], P('fsdp'), may hold values from -0.625 to 0.625
- exit_first_moment: float32 [768, 768], P('fsdp'), may hold values from -2.0861626e-07 to 2.0861626e-07
- exit_raw_moment: float32 [768, 768], P('fsdp'), may hold values from 9.7844415e-17 to 3.9137766e-16
- widening_matrix_in: float32 [768, 3072], P('fsdp'), may hold values from -0.21875 to 0.21875
- widening_first_moment: float32 [768, 3072], P('fsdp'), may hold values from -2.0861626e-07 to 2.0861626e-07
- widening_raw_moment: float32 [768, 3072], P('fsdp'), may hold values from 9.7844415e-17 to 3.9137766e-16
- narrowing_matrix_out: float32 [3072, 768], P('fsdp'), may hold values from -0.109375 to 0.109375
- narrowing_first_moment: float32 [3072, 768], P('fsdp'), may hold values from -4.4703484e-08 to 4.4703484e-08
- narrowing_raw_moment: float32 [3072, 768], P('fsdp'), may hold values from 3.9137765e-18 to 1.5655106e-17
- layernorm_scale_bias: float32 [4, 768], P(None, 'fsdp'), may hold values from -1.2 to 1.4, as said below
- layernorm_first_moment: float32 [4, 768], P(None, 'fsdp'), may hold values from -1.1920929e-06 to 1.1920929e-06
- layernorm_raw_moment: float32 [4, 768], P(None, 'fsdp'), may hold values from 3.51888e-15 to 1.407552e-14
Outputs:
- contrast_objective: float32 [], replicated
- grad_norm: float32 [], replicated
- embedding_out: float32 [4101, 768], P(None, 'fsdp')
- embed_first_out: float32 [4101, 768], P(None, 'fsdp')
- embed_second_out: float32 [4101, 768], P(None, 'fsdp')
- project_in_out: float32 [768, 2304], P('fsdp')
- in_first_out: float32 [768, 2304], P('fsdp')
- in_second_out: float32 [768, 2304], P('fsdp')
- project_out_out: float32 [768, 768], P('fsdp')
- out_first_out: float32 [768, 768], P('fsdp')
- out_second_out: float32 [768, 768], P('fsdp')
- ffn_up_out: float32 [768, 3072], P('fsdp')
- up_first_out: float32 [768, 3072], P('fsdp')
- up_second_out: float32 [768, 3072], P('fsdp')
- ffn_down_out: float32 [3072, 768], P('fsdp')
- down_first_out: float32 [3072, 768], P('fsdp')
- down_second_out: float32 [3072, 768], P('fsdp')
- norm_params_out: float32 [4, 768], P(None, 'fsdp')
- norm_first_out: float32 [4, 768], P(None, 'fsdp')
- norm_second_out: float32 [4, 768], P(None, 'fsdp')
Inputs may be any that keep to these rules, and one draw needn't show every extreme that they name: `slot_fragment_ids`: within a row the segment numbers never fall; numbers 0 to 31 are fragments, 32 is the row's padding tail; each has 1 to 32 slots, and some has exactly 32. Fragments are paired: mirror_fragment_index[mirror_fragment_index[i]] = i and mirror_fragment_index[i] != i. `fragment_weight`: positive weights. `layernorm_scale_bias`: rows 0 and 2 are the two norms' gains, rows 1 and 3 their shifts.
All inputs are finite; a program needn't handle non-finite values.
Results may differ from a plain program's by a relative error of at most 0.015.
Values may be sent and summed in bfloat16 or wider, within the bound.
No kernel may reach another device: no remote copies, remote signals or barrier semaphores. Data moves between devices by JAX's collectives and lax.ppermute only.
A program may use at most 256 MiB of HBM per device.

v0:
```python
import jax
import jax.numpy as jnp
from jax import lax
from jax.sharding import PartitionSpec as P

MODEL_WIDTH = 768
H = 12
HD = 64
SEG_ROW = 32


largest_value = lax.Precision.HIGHEST
beta_one = 0.9
beta_two = 0.999
adam_eps = 1e-12
decay_rate = 0.01
rate_matrix = 0.1
rate_embed = 1.0
rate_norm = 1.0
clip_norm = 0.001
norm_eps = 1e-05
unit_eps = 1e-06


def layer_norm(inputs, gain_row, shifts):
    center = inputs - jnp.mean(inputs, -1, keepdims=True)
    inv_std = lax.rsqrt(jnp.mean(center * center, -1, keepdims=True) + norm_eps)
    normed = center * inv_std
    return (normed * gain_row + shifts, normed, inv_std)


def norm_back(upstream, normed, inv_std, gain_row):
    scaled = upstream * gain_row
    grad_in = inv_std * (
        scaled
        - jnp.mean(scaled, -1, keepdims=True)
        - normed * jnp.mean(scaled * normed, -1, keepdims=True)
    )
    return (grad_in, jnp.sum(upstream * normed, 0), jnp.sum(upstream, 0))


def masked_scores(query_rows, key_rows, segment_rows):
    raw_scores = jnp.einsum(
        "bqhd,bkhd->bhqk", query_rows, key_rows, preferred_element_type=jnp.float32
    )
    same_segment = segment_rows[:, None, :, None] == segment_rows[:, None, None, :]
    return jnp.where(same_segment, raw_scores * HD ** (-0.5), -1e30)


def layer_forward(gathered, token_rows, segment_rows):
    (
        lexicon_table,
        query_key_value_maps,
        attention_exit_map,
        widening_matrix_in,
        narrowing_matrix_out,
        layernorm_scale_bias,
    ) = gathered
    batch_row_list, sequence_length = token_rows.shape
    embedded = jnp.take(lexicon_table, token_rows.reshape(-1), axis=0)
    qkv_all = jnp.dot(embedded, query_key_value_maps, preferred_element_type=jnp.float32).astype(
        jnp.bfloat16
    )
    qkv_all = qkv_all.reshape(batch_row_list, sequence_length, 3, H, HD)
    query_rows, key_rows, value_rows = (qkv_all[:, :, 0], qkv_all[:, :, 1], qkv_all[:, :, 2])
    scores = masked_scores(query_rows, key_rows, segment_rows)
    row_max = jnp.max(scores, -1, keepdims=True)
    log_total = row_max + jnp.log(jnp.sum(jnp.exp(scores - row_max), -1, keepdims=True))
    attn_probs = jnp.exp(scores - log_total).astype(jnp.bfloat16)
    mixed_heads = jnp.einsum(
        "bhqk,bkhd->bqhd", attn_probs, value_rows, preferred_element_type=jnp.float32
    )
    mixed_heads = mixed_heads.reshape(batch_row_list * sequence_length, MODEL_WIDTH).astype(
        jnp.bfloat16
    )
    attended = jnp.dot(mixed_heads, attention_exit_map, preferred_element_type=jnp.float32)
    normed_one, unit_one, inv_one = layer_norm(
        embedded.astype(jnp.float32) + attended, layernorm_scale_bias[0], layernorm_scale_bias[1]
    )
    normed_low = normed_one.astype(jnp.bfloat16)
    up_proj = jnp.dot(normed_low, widening_matrix_in, preferred_element_type=jnp.float32)
    activated = jax.nn.gelu(up_proj, approximate=False).astype(jnp.bfloat16)
    ffn_result = jnp.dot(activated, narrowing_matrix_out, preferred_element_type=jnp.float32)
    second_normalized, unit_two, inv_two = layer_norm(
        normed_one + ffn_result, layernorm_scale_bias[2], layernorm_scale_bias[3]
    )
    group_member = (
        segment_rows[:, None, :] == jnp.arange(SEG_ROW, dtype=jnp.int32)[None, :, None]
    ).astype(jnp.float32)
    pooled_state = jnp.einsum(
        "nkz,nzh->nkh",
        group_member,
        second_normalized.reshape(batch_row_list, sequence_length, MODEL_WIDTH),
        precision=largest_value,
    )
    saved_state = (
        embedded,
        query_rows,
        key_rows,
        value_rows,
        log_total,
        mixed_heads,
        unit_one,
        inv_one,
        normed_low,
        up_proj,
        activated,
        unit_two,
        inv_two,
        group_member,
    )
    return (pooled_state.reshape(batch_row_list * SEG_ROW, MODEL_WIDTH), saved_state)


def layer_backward(gathered, saved_state, token_rows, segment_rows, pooled_gradient):
    (
        lexicon_table,
        query_key_value_maps,
        attention_exit_map,
        widening_matrix_in,
        narrowing_matrix_out,
        layernorm_scale_bias,
    ) = gathered
    (
        embedded,
        query_rows,
        key_rows,
        value_rows,
        log_total,
        mixed_heads,
        unit_one,
        inv_one,
        normed_low,
        up_proj,
        activated,
        unit_two,
        inv_two,
        group_member,
    ) = saved_state
    batch_row_list, sequence_length = token_rows.shape
    pooled_gradient = pooled_gradient.reshape(batch_row_list, SEG_ROW, MODEL_WIDTH)
    second_gradient = jnp.einsum(
        "got,goy->gty", group_member, pooled_gradient, precision=largest_value
    ).reshape(batch_row_list * sequence_length, MODEL_WIDTH)
    grad_resid_two, grad_gain_two, grad_shift_two = norm_back(
        second_gradient, unit_two, inv_two, layernorm_scale_bias[2]
    )
    grad_result = grad_resid_two.astype(jnp.bfloat16)
    grad_ffn_down = jnp.einsum(
        "nf,nd->fd", activated, grad_result, preferred_element_type=jnp.float32
    )
    grad_act = jnp.einsum(
        "nd,fd->nf", grad_result, narrowing_matrix_out, preferred_element_type=jnp.float32
    )
    gelu_value, gelu_pull = jax.vjp(
        lambda pre_act: jax.nn.gelu(pre_act, approximate=False), up_proj
    )
    grad_up = gelu_pull(grad_act)[0].astype(jnp.bfloat16)
    grad_ffn_up = jnp.einsum("nd,nf->df", normed_low, grad_up, preferred_element_type=jnp.float32)
    grad_one = grad_resid_two + jnp.einsum(
        "nf,df->nd", grad_up, widening_matrix_in, preferred_element_type=jnp.float32
    )
    grad_resid_one, grad_gain_one, grad_shift_one = norm_back(
        grad_one, unit_one, inv_one, layernorm_scale_bias[0]
    )
    grad_attended = grad_resid_one.astype(jnp.bfloat16)
    grad_project_out = jnp.einsum(
        "nc,nd->cd", mixed_heads, grad_attended, preferred_element_type=jnp.float32
    )
    grad_mixed = jnp.einsum(
        "nd,cd->nc", grad_attended, attention_exit_map, preferred_element_type=jnp.float32
    )
    grad_mixed = grad_mixed.astype(jnp.bfloat16).reshape(batch_row_list, sequence_length, H, HD)
    scores = masked_scores(query_rows, key_rows, segment_rows)
    attn_probs = jnp.exp(scores - log_total)
    probs_low = attn_probs.astype(jnp.bfloat16)
    grad_values = jnp.einsum(
        "bhqk,bqhd->bkhd", probs_low, grad_mixed, preferred_element_type=jnp.float32
    )
    grad_probs = jnp.einsum(
        "bqhd,bkhd->bhqk", grad_mixed, value_rows, preferred_element_type=jnp.float32
    )
    grad_scores = attn_probs * (grad_probs - jnp.sum(grad_probs * attn_probs, -1, keepdims=True))
    grad_scores = grad_scores.astype(jnp.bfloat16)
    grad_query = jnp.einsum(
        "bhqk,bkhd->bqhd", grad_scores, key_rows, preferred_element_type=jnp.float32
    ) * HD ** (-0.5)
    grad_keys = jnp.einsum(
        "bhqk,bqhd->bkhd", grad_scores, query_rows, preferred_element_type=jnp.float32
    ) * HD ** (-0.5)
    grad_qkv = (
        jnp.stack([grad_query, grad_keys, grad_values], 2)
        .reshape(batch_row_list * sequence_length, 3 * MODEL_WIDTH)
        .astype(jnp.bfloat16)
    )
    grad_project_in = jnp.einsum(
        "nd,nc->dc", embedded, grad_qkv, preferred_element_type=jnp.float32
    )
    grad_embedded = grad_resid_one + jnp.einsum(
        "nc,dc->nd", grad_qkv, query_key_value_maps, preferred_element_type=jnp.float32
    )
    grad_norms = jnp.stack([grad_gain_one, grad_shift_one, grad_gain_two, grad_shift_two])
    return (
        grad_embedded,
        grad_project_in,
        grad_project_out,
        grad_ffn_up,
        grad_ffn_down,
        grad_norms,
    )


def adam_update(weight, first, second, grad, fix_first, fix_second, rate, decay):
    first_new = beta_one * first + (1.0 - beta_one) * grad
    second_new = beta_two * second + (1.0 - beta_two) * grad * grad
    step_size = first_new / fix_first / (jnp.sqrt(second_new / fix_second) + adam_eps)
    return (weight - rate * (step_size + decay * weight), first_new, second_new)


def per_device(
    kmer_identifiers,
    slot_fragment_ids,
    mirror_fragment_index,
    fragment_weight,
    affinity_heat,
    optimizer_iteration,
    lexicon_table,
    lexicon_first_moment,
    lexicon_raw_moment,
    query_key_value_maps,
    qkv_first_moment,
    qkv_raw_moment,
    attention_exit_map,
    exit_first_moment,
    exit_raw_moment,
    widening_matrix_in,
    widening_first_moment,
    widening_raw_moment,
    narrowing_matrix_out,
    narrowing_first_moment,
    narrowing_raw_moment,
    layernorm_scale_bias,
    layernorm_first_moment,
    layernorm_raw_moment,
):
    masters = (
        lexicon_table,
        query_key_value_maps,
        attention_exit_map,
        widening_matrix_in,
        narrowing_matrix_out,
        layernorm_scale_bias,
    )
    firsts = (
        lexicon_first_moment,
        qkv_first_moment,
        exit_first_moment,
        widening_first_moment,
        narrowing_first_moment,
        layernorm_first_moment,
    )
    seconds = (
        lexicon_raw_moment,
        qkv_raw_moment,
        exit_raw_moment,
        widening_raw_moment,
        narrowing_raw_moment,
        layernorm_raw_moment,
    )
    rates = (rate_embed, rate_matrix, rate_matrix, rate_matrix, rate_matrix, rate_norm)
    decays = (decay_rate, decay_rate, decay_rate, decay_rate, decay_rate, 0.0)
    lowered = tuple((piece.astype(jnp.bfloat16) for piece in masters))
    gathered = (
        lax.all_gather(lowered[0], "fsdp", axis=1, tiled=True),
        lax.all_gather(lowered[1], "fsdp", axis=0, tiled=True),
        lax.all_gather(lowered[2], "fsdp", axis=0, tiled=True),
        lax.all_gather(lowered[3], "fsdp", axis=0, tiled=True),
        lax.all_gather(lowered[4], "fsdp", axis=0, tiled=True),
        lax.all_gather(lowered[5], "fsdp", axis=1, tiled=True),
    )
    pooled_state, saved_state = layer_forward(gathered, kmer_identifiers, slot_fragment_ids)
    unit_scale = lax.rsqrt(jnp.sum(pooled_state * pooled_state, -1, keepdims=True) + unit_eps)
    unit_rows = pooled_state * unit_scale
    unit_low = unit_rows.astype(jnp.bfloat16)
    every_unit = lax.all_gather(unit_low, ("fsdp", "dp"), axis=0, tiled=True)
    cosine_affinity_grid = jnp.einsum(
        "sd,td->st", unit_low, every_unit, preferred_element_type=jnp.float32
    )
    seg_local = pooled_state.shape[0]
    fragment_tally = every_unit.shape[0]
    shard_fragment_lines = lax.axis_index(("fsdp", "dp")) * seg_local + jnp.arange(
        seg_local, dtype=jnp.int32
    )
    field_sequence_array = jnp.arange(fragment_tally, dtype=jnp.int32)
    raw_affinity_values = jnp.where(
        shard_fragment_lines[:, None] == field_sequence_array[None, :],
        -1e30,
        cosine_affinity_grid / affinity_heat,
    )
    row_max = jnp.max(raw_affinity_values, -1, keepdims=True)
    log_total = row_max[:, 0] + jnp.log(jnp.sum(jnp.exp(raw_affinity_values - row_max), -1))
    chosen = mirror_fragment_index[:, None] == field_sequence_array[None, :]
    chosen_real_entry = chosen.astype(jnp.float32)
    target = jnp.sum(jnp.where(chosen, raw_affinity_values, 0.0), -1)
    contrast_objective = (
        lax.psum(jnp.sum(fragment_weight * (log_total - target)), ("fsdp", "dp")) / fragment_tally
    )
    exponent_probabilities = jnp.exp(raw_affinity_values - log_total[:, None])
    similarity_gradient = (
        (exponent_probabilities - chosen_real_entry)
        * fragment_weight[:, None]
        / (fragment_tally * affinity_heat)
    ).astype(jnp.bfloat16)
    grad_rows = jnp.dot(similarity_gradient, every_unit, preferred_element_type=jnp.float32)
    column_terms = jnp.einsum(
        "st,sd->td", similarity_gradient, unit_low, preferred_element_type=jnp.float32
    )
    grad_cols = lax.psum_scatter(column_terms, ("fsdp", "dp"), scatter_dimension=0, tiled=True)
    grad_unit = grad_rows + grad_cols
    pooled_gradient = unit_scale * (
        grad_unit - unit_rows * jnp.sum(grad_unit * unit_rows, -1, keepdims=True)
    )
    again = (
        lax.all_gather(lowered[0], "fsdp", axis=1, tiled=True),
        lax.all_gather(lowered[1], "fsdp", axis=0, tiled=True),
        lax.all_gather(lowered[2], "fsdp", axis=0, tiled=True),
        lax.all_gather(lowered[3], "fsdp", axis=0, tiled=True),
        lax.all_gather(lowered[4], "fsdp", axis=0, tiled=True),
        lax.all_gather(lowered[5], "fsdp", axis=1, tiled=True),
    )
    grads = layer_backward(again, saved_state, kmer_identifiers, slot_fragment_ids, pooled_gradient)
    vocab = lexicon_table.shape[0]
    rest = (
        lax.psum_scatter(grads[1], "fsdp", scatter_dimension=0, tiled=True),
        lax.psum_scatter(grads[2], "fsdp", scatter_dimension=0, tiled=True),
        lax.psum_scatter(grads[3], "fsdp", scatter_dimension=0, tiled=True),
        lax.psum_scatter(grads[4], "fsdp", scatter_dimension=0, tiled=True),
        lax.psum_scatter(grads[5], "fsdp", scatter_dimension=1, tiled=True),
    )
    column_rows = lax.all_to_all(
        grads[0].astype(jnp.bfloat16), "fsdp", split_axis=1, concat_axis=0, tiled=True
    ).astype(jnp.float32)
    all_tokens = lax.all_gather(kmer_identifiers.reshape(-1), "fsdp", axis=0, tiled=True)
    table_shard = jax.ops.segment_sum(column_rows, all_tokens, num_segments=vocab)
    shards = (table_shard, rest[0], rest[1], rest[2], rest[3], rest[4])
    shards = (
        lax.psum(shards[0].astype(jnp.bfloat16), "dp").astype(jnp.float32),
        lax.psum(shards[1].astype(jnp.bfloat16), "dp").astype(jnp.float32),
        lax.psum(shards[2].astype(jnp.bfloat16), "dp").astype(jnp.float32),
        lax.psum(shards[3].astype(jnp.bfloat16), "dp").astype(jnp.float32),
        lax.psum(shards[4].astype(jnp.bfloat16), "dp").astype(jnp.float32),
        lax.psum(shards[5].astype(jnp.bfloat16), "dp").astype(jnp.float32),
    )
    squares = sum((jnp.sum(piece * piece) for piece in shards))
    grad_norm = jnp.sqrt(lax.psum(squares, "fsdp"))
    factor = clip_norm / jnp.maximum(grad_norm, clip_norm)
    count_now = optimizer_iteration.astype(jnp.float32)
    fix_first = 1.0 - jnp.power(beta_one, count_now)
    fix_second = 1.0 - jnp.power(beta_two, count_now)
    updated = [
        adam_update(
            masters[number],
            firsts[number],
            seconds[number],
            shards[number] * factor,
            fix_first,
            fix_second,
            rates[number],
            decays[number],
        )
        for number in range(6)
    ]
    return (
        contrast_objective,
        grad_norm,
        updated[0][0],
        updated[0][1],
        updated[0][2],
        updated[1][0],
        updated[1][1],
        updated[1][2],
        updated[2][0],
        updated[2][1],
        updated[2][2],
        updated[3][0],
        updated[3][1],
        updated[3][2],
        updated[4][0],
        updated[4][1],
        updated[4][2],
        updated[5][0],
        updated[5][1],
        updated[5][2],
    )


def solution(mesh):
    in_specs = (
        P(("fsdp", "dp"), None),
        P(("fsdp", "dp"), None),
        P(("fsdp", "dp")),
        P(("fsdp", "dp")),
        P(),
        P(),
        P(None, "fsdp"),
        P(None, "fsdp"),
        P(None, "fsdp"),
        P("fsdp", None),
        P("fsdp", None),
        P("fsdp", None),
        P("fsdp", None),
        P("fsdp", None),
        P("fsdp", None),
        P("fsdp", None),
        P("fsdp", None),
        P("fsdp", None),
        P("fsdp", None),
        P("fsdp", None),
        P("fsdp", None),
        P(None, "fsdp"),
        P(None, "fsdp"),
        P(None, "fsdp"),
    )
    out_specs = (
        P(),
        P(),
        P(None, "fsdp"),
        P(None, "fsdp"),
        P(None, "fsdp"),
        P("fsdp", None),
        P("fsdp", None),
        P("fsdp", None),
        P("fsdp", None),
        P("fsdp", None),
        P("fsdp", None),
        P("fsdp", None),
        P("fsdp", None),
        P("fsdp", None),
        P("fsdp", None),
        P("fsdp", None),
        P("fsdp", None),
        P(None, "fsdp"),
        P(None, "fsdp"),
        P(None, "fsdp"),
    )
    return jax.shard_map(
        per_device, mesh=mesh, in_specs=in_specs, out_specs=out_specs, check_vma=False
    )
```

profile of v0, /device:TPU:0, one launch (start us, length us, event | category | flops | bytes accessed | tf_op | source)
XLA Modules:
  0.0 1466.7 jit_solution(12044774444236617262)
XLA Ops:
  15.5 42.6 %all-gather.1 = bf16[16,48,4]{1,2,0:T(4,128)(2,1)S(1)} all-gather(bf16[1,48,4]{1,2,0:T(4,128)(2,1)S(1)} %convert_bitcast_fusion.1), channel_id=1, replica_groups=mesh['fsdp'=16,'dp'=2] {'fsdp'}, dimensions={0}, use_global_device_ids=true | all-gather | bytes 6528 | tf_op jit(solution)/shard_map/all_gather | solution.py:279
  58.5 51.8 %all-gather.9.cloned.1.call-done = bf16[4101,768]{0,1:T(8,128)(2,1)} async-done(((bf16[4101,48]{0,1:T(8,128)(2,1)}), bf16[4101,768]{0,1:T(8,128)(2,1)}) %all-gather.9.cloned.1.call-update) | async-done | bytes 6299152 | tf_op jit(solution)/shard_map/all_gather | solution.py:274
  110.4 9.3 copy.107
  125.8 57.4 %all-gather.11.cloned.1.call-done = bf16[768,2304]{1,0:T(8,128)(2,1)} async-done(((bf16[48,2304]{1,0:T(8,128)(2,1)}), bf16[768,2304]{1,0:T(8,128)(2,1)}) %all-gather.11.cloned.1.call-update) | async-done | bytes 3538960 | tf_op jit(solution)/shard_map/all_gather | solution.py:275
  202.2 39.2 %all-gather.13.cloned.1.call-done = bf16[768,768]{1,0:T(8,128)(2,1)} async-done(((bf16[48,768]{1,0:T(8,128)(2,1)}), bf16[768,768]{1,0:T(8,128)(2,1)}) %all-gather.13.cloned.1.call-update) | async-done | bytes 1179664 | tf_op jit(solution)/shard_map/all_gather | solution.py:276
  245.2 78.7 %all-gather.15.cloned.1.call-done = bf16[768,3072]{1,0:T(8,128)(2,1)} async-done(((bf16[48,3072]{1,0:T(8,128)(2,1)}), bf16[768,3072]{1,0:T(8,128)(2,1)}) %all-gather.15.cloned.1.call-update) | async-done | bytes 4718608 | tf_op jit(solution)/shard_map/all_gather | solution.py:277
  323.9 21.0 %multiply_convert_fusion.1 = (bf16[512,3072]{1,0:T(8,128)(2,1)}, f32[512,3072]{1,0:T(8,128)}, f32[512,3072]{1,0:T(8,128)}) fusion(bf16[768,3072]{1,0:T(8,128)(2,1)} %all-gather.15.cloned.1.call-done, f32[512,768]{1,0:T(8,128)} %copy-done.4, f32[768]{0:T(1024)S(1)} %get-tuple-element.92, f32[768]{0:T(1024)S(1)} %get-tuple-element.93, ...), kind=kOutput, calls=%fused_computation.12 | convolution fusion | flops 2520121344 | bytes 22030336 | tf_op jit(solution)/shard_map/dot_general | solution.py:81
  344.9 61.3 %all-gather.17.cloned.1.call-done = bf16[3072,768]{1,0:T(8,128)(2,1)} async-done(((bf16[192,768]{1,0:T(8,128)(2,1)}), bf16[3072,768]{1,0:T(8,128)(2,1)}) %all-gather.17.cloned.1.call-update) | async-done | bytes 4718608 | tf_op jit(solution)/shard_map/all_gather | solution.py:278
  416.3 53.0 %all-gather.19.cloned.1.call-done = bf16[1024,768]{1,0:T(8,128)(2,1)} async-done(((bf16[32,768]{1,0:T(8,128)(2,1)}), bf16[1024,768]{1,0:T(8,128)(2,1)}) %all-gather.19.cloned.1.call-update) | async-done | bytes 1572880 | tf_op jit(solution)/shard_map/all_gather | solution.py:285
  475.6 100.5 %reduce-scatter.9.cloned.1.call-done = f32[32,768]{1,0:T(8,128)} async-done(((f32[1024,768]{1,0:T(8,128)}), f32[32,768]{1,0:T(8,128)}) %reduce-scatter.9.cloned.1.call-update) | async-done | bytes 98320 | tf_op jit(solution)/shard_map/reduce_scatter | solution.py:318
  581.5 9.0 add_convert_fusion
  602.5 11.4 multiply_reduce_fusion
  615.1 7.0 multiply_convert_fusion
  634.7 8.9 fusion.78
  643.9 8.7 fusion.43
  663.1 45.8 %all-gather = s32[1,8192]{1,0:T(1,128)S(1)} all-gather(s32[1,512]{1,0:T(1,128)S(1)} %copy-done.29), channel_id=2, replica_groups=mesh['fsdp'=16,'dp'=2] {'fsdp'}, dimensions={1}, use_global_device_ids=true | all-gather | bytes 34816 | tf_op jit(solution)/shard_map/all_gather | solution.py:343
  713.0 44.8 %scatter_custom_fusion = f32[4101,48]{1,0:T(8,128)S(1)} fusion(s32[8192]{0:T(1024)S(1)} %bitcast.103, f32[8192,48]{1,0:T(8,128)} %bitcast.96, f32[]{:T(128)} %constant.64.clone.1), kind=kCustom, calls=%fused_computation.62 | custom fusion | flops 393216 | bytes 787904 | tf_op jit(solution)/shard_map/scatter-add | solution.py:344
  760.6 129.3 %reduce-scatter.11.cloned.1.call-done = f32[48,2304]{1,0:T(8,128)} async-done(((f32[768,2304]{1,0:T(8,128)}), f32[48,2304]{1,0:T(8,128)}) %reduce-scatter.11.cloned.1.call-update) | async-done | bytes 442384 | tf_op jit(solution)/shard_map/reduce_scatter | solution.py:334
  891.6 173.6 %reduce-scatter.15.cloned.1.call-done = f32[48,3072]{1,0:T(8,128)} async-done(((f32[768,3072]{1,0:T(8,128)}), f32[48,3072]{1,0:T(8,128)}) %reduce-scatter.15.cloned.1.call-update) | async-done | bytes 589840 | tf_op jit(solution)/shard_map/reduce_scatter | solution.py:336
  1067.0 173.7 %reduce-scatter.17.cloned.1.call-done = f32[192,768]{1,0:T(8,128)} async-done(((f32[3072,768]{1,0:T(8,128)}), f32[192,768]{1,0:T(8,128)}) %reduce-scatter.17.cloned.1.call-update) | async-done | bytes 589840 | tf_op jit(solution)/shard_map/reduce_scatter | solution.py:337
  1243.3 39.4 %psum.56 = f32[]{:T(128)} all-reduce(f32[]{:T(128)} %get-tuple-element.117), channel_id=1, replica_groups=mesh['fsdp'=16,'dp'=2] {'fsdp','dp'}, use_global_device_ids=true, to_apply=%region_11.12 | all-reduce | flops 1 | bytes 8 | tf_op jit(solution)/shard_map/psum | solution.py:306
  1282.7 84.0 %reduce-scatter.19.cloned.1.call-done = f32[48,4]{1,0:T(8,128)} async-done(((f32[768,4]{1,0:T(8,128)}), f32[48,4]{1,0:T(8,128)}) %reduce-scatter.19.cloned.1.call-update) | async-done | bytes 784
  1370.6 19.9 %all-reduce.3.cloned.1.call-done = (bf16[4101,48]{0,1:T(8,128)(2,1)}, bf16[48,2304]{1,0:T(8,128)(2,1)}, bf16[48,768]{1,0:T(8,128)(2,1)}, bf16[48,3072]{1,0:T(8,128)(2,1)}, bf16[192,768]{1,0:T(8,128)(2,1)}) async-done(((bf16[4101,48]{0,1:T(8,128)(2,1)}, bf16[48,2304]{1,0:T(8,128)(2,1)}, bf16[48,768]{1,0:T(8,128)(2,1)}, bf16[48,3072]{1,0:T(8,128)(2,1)}, bf16[192,768]{1,0:T(8,128)(2,1)}), ...) | async-done | bytes 1278448 | tf_op jit(solution)/shard_map/psum | solution.py:347
  1403.5 42.8 %psum.63 = f32[]{:T(128)} all-reduce(f32[]{:T(128)S(6)} %add.282), channel_id=1, replica_groups=mesh['fsdp'=16,'dp'=2] {'fsdp'}, use_global_device_ids=true, to_apply=%region_41.42 | all-reduce | flops 1 | bytes 8 | tf_op jit(solution)/shard_map/psum | solution.py:355
  (196 shorter events, 129.5 us)
Async XLA Ops:
  7.2 103.1 %all-gather.9.cloned.1.call-start = ((), (), s32[]{:S(2)}) async-start(), calls=%async_computation.7 | async-start | bytes 6893568 | tf_op jit(solution)/shard_map/all_gather | solution.py:274
  9.3 173.9 %all-gather.11.cloned.1.call-start = ((), (), s32[]{:S(2)}) async-start(), calls=%async_computation.8 | async-start | bytes 3760128 | tf_op jit(solution)/shard_map/all_gather | solution.py:275
  11.1 230.2 %all-gather.13.cloned.1.call-start = ((), (), s32[]{:S(2)}) async-start(), calls=%async_computation.9 | async-start | bytes 1253376 | tf_op jit(solution)/shard_map/all_gather | solution.py:276
  12.7 311.2 %all-gather.15.cloned.1.call-start = ((), (), s32[]{:S(2)}) async-start(), calls=%async_computation.10 | async-start | bytes 5013504 | tf_op jit(solution)/shard_map/all_gather | solution.py:277
  14.6 391.6 %all-gather.17.cloned.1.call-start = ((), (), s32[]{:S(2)}) async-start(), calls=%async_computation.11 | async-start | bytes 5013504 | tf_op jit(solution)/shard_map/all_gather | solution.py:278
  15.4 453.9 %all-gather.19.cloned.1.call-start = ((), (), s32[]{:S(2)}) async-start(), calls=%async_computation.12 | async-start | bytes 1622016 | tf_op jit(solution)/shard_map/all_gather | solution.py:285
  125.8 115.5 %copy-start.8 = (bf16[512,768]{1,0:T(8,128)(2,1)}, bf16[512,768]{1,0:T(8,128)(2,1)S(1)}, u32[]{:S(2)}) copy-start(bf16[512,768]{1,0:T(8,128)(2,1)S(1)} %gather_fusion) | copy-start | bytes 2359300
  412.7 58.8 %copy-start.32 = (s32[32]{0:T(128)S(1)}, s32[32]{0:T(128)}, u32[]{:S(2)}) copy-start(s32[32]{0:T(128)} %param.26) | copy-start | bytes 388
  412.7 59.0 %copy-start.33 = (f32[32]{0:T(128)S(1)}, f32[32]{0:T(128)}, u32[]{:S(2)}) copy-start(f32[32]{0:T(128)} %param.27) | copy-start | bytes 388
  415.6 160.4 %reduce-scatter.9.cloned.1.call-start = ((), (), s32[]{:S(2)}) async-start(), calls=%async_computation.13 | async-start | bytes 3244032 | tf_op jit(solution)/shard_map/reduce_scatter | solution.py:318
  475.5 283.5 %reduce-scatter.13.cloned.1.call-start = ((), (), s32[]{:S(2)}) async-start(), calls=%async_computation.15 | async-start | bytes 2506752 | tf_op jit(solution)/shard_map/reduce_scatter | solution.py:335
  602.4 287.5 %reduce-scatter.11.cloned.1.call-start = ((), (), s32[]{:S(2)}) async-start(), calls=%async_computation.14 | async-start | bytes 7520256 | tf_op jit(solution)/shard_map/reduce_scatter | solution.py:334
  634.7 430.5 %reduce-scatter.15.cloned.1.call-start = ((), (), s32[]{:S(2)}) async-start(), calls=%async_computation.16 | async-start | bytes 10027008 | tf_op jit(solution)/shard_map/reduce_scatter | solution.py:336
  643.7 597.0 %reduce-scatter.17.cloned.1.call-start = ((), (), s32[]{:S(2)}) async-start(), calls=%async_computation.17 | async-start | bytes 10027008 | tf_op jit(solution)/shard_map/reduce_scatter | solution.py:337
  658.4 51.6 %all-to-all-start = ((bf16[512,16,48]{0,2,1:T(8,128)(2,1)}), bf16[512,16,48]{0,2,1:T(8,128)(2,1)S(1)}, u32[]{:S(2)}, u32[]{:S(2)}) async-start(bf16[512,16,48]{0,2,1:T(8,128)(2,1)} %bitcast.26), calls=%async_computation.1 | async-start | bytes 1572864 | tf_op jit(solution)/shard_map/all_to_all | solution.py:340
  663.1 703.6 %reduce-scatter.19.cloned.1.call-start = ((), (), s32[]{:S(2)}) async-start(), calls=%async_computation.18 | async-start | bytes 417792
  710.0 680.5 %all-reduce.3.cloned.1.call-start = ((), (), s32[]{:S(2)}) async-start(), calls=%async_computation.19 | async-start | bytes 2580480 | tf_op jit(solution)/shard_map/psum | solution.py:347
  757.8 689.1 %copy-start.31 = (f32[4,48]{1,0:T(4,128)S(1)}, f32[4,48]{1,0:T(4,128)}, u32[]{:S(2)}) copy-start(f32[4,48]{1,0:T(4,128)} %param.45) | copy-start | bytes 2308
  757.9 689.1 %copy-start.34 = (f32[4,48]{1,0:T(4,128)S(1)}, f32[4,48]{1,0:T(4,128)}, u32[]{:S(2)}) copy-start(f32[4,48]{1,0:T(4,128)} %param.47) | copy-start | bytes 2308
  757.9 689.1 %copy-start.35 = (f32[4,48]{1,0:T(4,128)S(1)}, f32[4,48]{1,0:T(4,128)}, u32[]{:S(2)}) copy-start(f32[4,48]{1,0:T(4,128)} %param.46) | copy-start | bytes 2308
  757.9 689.7 %copy-start.11 = (f32[192,768]{1,0:T(8,128)S(1)}, f32[192,768]{1,0:T(8,128)}, u32[]{:S(2)}) copy-start(f32[192,768]{1,0:T(8,128)} %param.42) | copy-start | bytes 1769476
  757.9 689.7 %copy-start.21 = (f32[192,768]{1,0:T(8,128)S(1)}, f32[192,768]{1,0:T(8,128)}, u32[]{:S(2)}) copy-start(f32[192,768]{1,0:T(8,128)} %param.44) | copy-start | bytes 1769476
  1067.0 383.5 %copy-start.12 = (f32[48,3072]{1,0:T(8,128)S(1)}, f32[48,3072]{1,0:T(8,128)}, u32[]{:S(2)}) copy-start(f32[48,3072]{1,0:T(8,128)} %param.39) | copy-start | bytes 1769476
  1390.5 60.0 %copy-start.15 = (bf16[48,3072]{1,0:T(8,128)(2,1)S(1)}, bf16[48,3072]{1,0:T(8,128)(2,1)}, u32[]{:S(2)}) copy-start(bf16[48,3072]{1,0:T(8,128)(2,1)} %get-tuple-element.97) | copy-start | bytes 884740
  (32 other events, 246.5 us)
Sparse Core Ops, SparseCore 0:
  11.4 98.8 all-gather.8
  113.7 69.4 all-gather.10
  186.6 54.6 all-gather.12
  244.5 79.3 all-gather.14
  327.1 79.0 all-gather.16
  415.8 53.5 all-gather.18
  475.6 100.3 reduce-scatter.8
  602.5 130.7 reduce-scatter.12
  739.5 150.3 reduce-scatter.10
  896.3 168.8 reduce-scatter.14
  1070.9 169.7 reduce-scatter.16
  1246.5 120.1 reduce-scatter.18
  1371.1 19.3 all-reduce.2
where the time goes:
time: 1480 us; the launch traced here: 1470 us
  waiting for transfers between devices  1020 us (69%)
  blocking collectives  173 us (12%)
  matrix products  115 us (8%)
  other arithmetic  92.3 us (6%)
  local copies, waits for them, and re-layouts  34.1 us (2%)
  between operations  24 us (2%)
    reduce_scatter x1, waiting for transfers between devices, per_device(): lax.psum_scatter(grads[4], 'fsdp', scatter_dimension=0, tiled=True)  174 us
    reduce_scatter x1, waiting for transfers between devices, per_device(): lax.psum_scatter(grads[3], 'fsdp', scatter_dimension=0, tiled=True)  174 us
    reduce_scatter x1, waiting for transfers between devices, per_device(): lax.psum_scatter(grads[1], 'fsdp', scatter_dimension=0, tiled=True)  129 us
    reduce_scatter x1, waiting for transfers between devices, per_device(): lax.psum_scatter(column_terms, ('fsdp', 'dp'), scatter_dimension=0, tiled...  100 us
    unnamed x14, waiting for transfers between devices  84.3 us
    all_gather x1, waiting for transfers between devices, per_device(): lax.all_gather(lowered[3], 'fsdp', axis=0, tiled=True)  78.7 us
    all_gather x1, waiting for transfers between devices, per_device(): lax.all_gather(lowered[4], 'fsdp', axis=0, tiled=True)  61.3 us
    all_gather x1, waiting for transfers between devices, per_device(): lax.all_gather(lowered[1], 'fsdp', axis=0, tiled=True)  57.4 us
  transfers between devices with their start and end apart: 14, of which 12 were waited for; matrix products, arithmetic and copies ran while one was open for 12% of the time, Pallas kernels for 0%

commit v1 on v0

--- a/solution.py
+++ b/solution.py
@@ -1,6 +1,8 @@
 import jax
 import jax.numpy as jnp
 from jax import lax
+from jax.experimental import pallas as pl
+from jax.experimental.pallas import tpu as pltpu
 from jax.sharding import PartitionSpec as P
 
 MODEL_WIDTH = 768
@@ -394,6 +396,1310 @@
     )
 
 
+AXES = ("fsdp", "dp")
+VOCAB_PAD = 4352
+VOCAB_HALF = VOCAB_PAD // 2
+BIG_VMEM = pltpu.CompilerParams(vmem_limit_bytes=60 * 1024 * 1024)
+bf16 = jnp.bfloat16
+f32 = jnp.float32
+
+
+def pairs_of(moved):
+    spots = [(z, y, x, c) for z in range(4) for y in range(2) for x in range(2) for c in range(2)]
+
+    def linear(spot):
+        z, y, x, c = spot
+        return ((z * 2 + y) * 2 + x) * 2 + c
+
+    return [(linear(spot), linear(moved(*spot))) for spot in spots]
+
+
+FIRST = pairs_of(lambda z, y, x, c: (z, y, x ^ 1, c) if c == 0 else (z, y ^ 1, x, c))
+SECOND = pairs_of(lambda z, y, x, c: (z, y ^ 1, x, c) if c == 0 else (z, y, x ^ 1, c))
+BOTH = pairs_of(lambda z, y, x, c: (z, y ^ 1, x ^ 1, c))
+CORE = pairs_of(lambda z, y, x, c: (z, y, x, 1 - c))
+ZS = [None] + [pairs_of(lambda z, y, x, c, j=j: (z ^ j, y, x, c)) for j in (1, 2, 3)]
+
+
+def send(array, pairs):
+    return lax.ppermute(array, AXES, pairs)
+
+
+def after(array, *others):
+    return lax.optimization_barrier((array,) + others)[0]
+
+
+def together(arrays, *others):
+    arrays = list(arrays)
+    return list(lax.optimization_barrier((*arrays, *others)))[: len(arrays)]
+
+
+class Place:
+    def __init__(self):
+        f = lax.axis_index("fsdp")
+        self.core = lax.axis_index("dp")
+        self.z, self.y, self.x = f // 4, (f // 2) % 2, f % 2
+
+    def plane_slot(self, core, a, b):
+        dy = jnp.where(core == 0, b, a)
+        dx = jnp.where(core == 0, a, b)
+        return (self.y ^ dy) * 2 + (self.x ^ dx)
+
+    def chip(self, core, j, a, b):
+        return (self.z ^ j) * 4 + self.plane_slot(core, a, b)
+
+
+def z_sends(piece):
+    return [piece] + [send(piece, ZS[j]) for j in (1, 2, 3)]
+
+
+def z_column(piece):
+    return jnp.stack(z_sends(piece))
+
+
+def plane_sends(column, direct=False, gate=()):
+    one = send(column, FIRST)
+    two = send(column, SECOND)
+    three = send(column, BOTH) if direct else send(after(one, *gate), SECOND)
+    return [column, one, two, three]
+
+
+def both_cores(mine):
+    return mine + [send(block, CORE) for block in mine]
+
+
+def piece_index(place, rows):
+    halves, starts = [], []
+    for core in (place.core, 1 - place.core):
+        for a, b in ((0, 0), (1, 0), (0, 1), (1, 1)):
+            for j in range(4):
+                halves.append(core)
+                starts.append(place.chip(core, j, a, b) * rows)
+    return jnp.stack(halves + starts).astype(jnp.int32)
+
+
+def slot_index(place):
+    chips = [
+        place.chip(place.core, j, a, b) for b in (0, 1) for a in (0, 1) for j in range(4)
+    ]
+    return jnp.stack(chips).astype(jnp.int32)
+
+
+def scatter_add(keep, came):
+    return (keep[4:].astype(f32) + came[4:].astype(f32)).astype(bf16)
+
+
+def scatter_here(keep, came, came_two):
+    here = [
+        keep[j].astype(f32) + came[j].astype(f32) + came_two[j].astype(f32) for j in range(4)
+    ]
+    return here[0], [h.astype(bf16) for h in here[1:]]
+
+
+def line_sends(far):
+    return [send(h, ZS[j]) for h, j in zip(far, (1, 2, 3))]
+
+
+def line_sum(here, far):
+    return (here + far[0].astype(f32) + far[1].astype(f32) + far[2].astype(f32)).astype(bf16)
+
+
+def whole_copies(sources, targets, sems):
+    return [
+        pltpu.make_async_copy(source, target, sems.at[number])
+        for number, (source, target) in enumerate(zip(sources, targets))
+    ]
+
+
+def staged_call(body, scalars, arrays, pieces, shapes, scratch, cost):
+    n_s, n_a, n_p, n_o = len(scalars), len(arrays), len(pieces), len(shapes)
+
+    def kernel(*refs):
+        smem, refs = refs[:n_s], refs[n_s:]
+        hbm, refs = refs[:n_a], refs[n_a:]
+        far, refs = refs[:n_p], refs[n_p:]
+        out, refs = refs[:n_o], refs[n_o:]
+        near_in, refs = refs[:n_a], refs[n_a:]
+        near_out, refs = refs[:n_o], refs[n_o:]
+        in_sems, out_sems, refs = refs[0], refs[1], refs[2:]
+        copies = whole_copies(hbm, near_in, in_sems)
+        for copy in copies:
+            copy.start()
+
+        def ready():
+            for copy in copies:
+                copy.wait()
+
+        body(ready, *smem, *near_in, *far, *near_out, *refs)
+        copies_out = whole_copies(near_out, out, out_sems)
+        for copy in copies_out:
+            copy.start()
+        for copy in copies_out:
+            copy.wait()
+
+    in_hbm = pl.BlockSpec(memory_space=pltpu.HBM)
+    return pl.pallas_call(
+        kernel,
+        out_shape=shapes,
+        in_specs=[pl.BlockSpec(memory_space=pltpu.SMEM)] * n_s + [in_hbm] * (n_a + n_p),
+        out_specs=[in_hbm] * n_o,
+        scratch_shapes=[pltpu.VMEM(a.shape, a.dtype) for a in arrays]
+        + [pltpu.VMEM(s.shape, s.dtype) for s in shapes]
+        + [pltpu.SemaphoreType.DMA((n_a,)), pltpu.SemaphoreType.DMA((n_o,))]
+        + scratch,
+        cost_estimate=pl.CostEstimate(flops=int(cost * 1e9), bytes_accessed=0, transcendentals=0),
+        compiler_params=BIG_VMEM,
+    )(*scalars, *arrays, *pieces)
+
+
+def shaped(dtype, *dims):
+    return jax.ShapeDtypeStruct(dims, dtype)
+
+
+def one_hot(ids_row, start, count):
+    spots = lax.broadcasted_iota(jnp.int32, (count, ids_row.shape[1]), 0) + start
+    return jnp.where(spots == ids_row, 1.0, 0.0).astype(bf16)
+
+
+def lookup_kernel(ready, idx_ref, ids_ref, *refs):
+    ins = list(refs[:4]) + [refs[4].at[k] for k in range(3)]
+    outs, table, sems = refs[5:9], refs[9], refs[10]
+    copies = [
+        pltpu.make_async_copy(
+            ins[0], table.at[pl.ds(pl.multiple_of(idx_ref[0], 16), 48), :], sems.at[0]
+        )
+    ]
+    for number in range(1, 7):
+        column = pl.multiple_of(idx_ref[7 + (number - 1) // 3], 128)
+        row = pl.multiple_of(idx_ref[number], 16)
+        copies.append(
+            pltpu.make_async_copy(
+                ins[number],
+                table.at[pl.ds(row, 48), pl.ds(column, VOCAB_HALF)],
+                sems.at[number],
+            )
+        )
+    for copy in copies:
+        copy.start()
+    ready()
+    for copy in copies:
+        copy.wait()
+    for j in range(4):
+        total = jnp.zeros((192, 512), f32)
+        for k in range(VOCAB_PAD // 256):
+            total += jnp.dot(
+                table[:, k * 256 : (k + 1) * 256],
+                one_hot(ids_ref[j], k * 256, 256),
+                preferred_element_type=f32,
+            )
+        outs[j][...] = total.astype(bf16)
+
+
+def lookup(index, ids_z, arrays):
+    return staged_call(
+        lookup_kernel,
+        [index],
+        [ids_z],
+        arrays,
+        [
+            shaped(bf16, 192, 512),
+            shaped(bf16, 192, 512),
+            shaped(bf16, 192, 512),
+            shaped(bf16, 192, 512),
+        ],
+        [
+            pltpu.VMEM((192, VOCAB_PAD), bf16),
+            pltpu.SemaphoreType.DMA((7,)),
+        ],
+        6,
+    )
+
+
+def token_sum_kernel(ready, idx_ref, ids_ref, other_ids_ref, mine_ref, other_ref, keep_ref, away_ref, whole_ref
+):
+    ready()
+    start = idx_ref[0]
+    for low in range(0, VOCAB_HALF, 256):
+        count = min(256, VOCAB_HALF - low)
+        total = jnp.zeros((192, count), f32)
+        for ids, block in ((ids_ref, mine_ref), (other_ids_ref, other_ref)):
+            for j in range(4):
+                total += lax.dot_general(
+                    block[j],
+                    one_hot(ids[j], start + low, count),
+                    (((1,), (1,)), ((), ())),
+                    preferred_element_type=f32,
+                )
+        whole_ref[:, low : low + count] = total.astype(bf16)
+    for k in range(2):
+        keep_ref[k] = whole_ref[pl.ds(pl.multiple_of(idx_ref[1 + k], 16), 48), :]
+        away_ref[k] = whole_ref[pl.ds(pl.multiple_of(idx_ref[3 + k], 16), 48), :]
+
+
+def token_sum(index, ids_z, other_ids, mine, other):
+    return staged_call(
+        token_sum_kernel,
+        [index],
+        [ids_z, other_ids, mine, other],
+        [],
+        [
+            shaped(bf16, 2, 48, VOCAB_HALF),
+            shaped(bf16, 2, 48, VOCAB_HALF),
+        ],
+        [
+            pltpu.VMEM((192, VOCAB_HALF), bf16),
+        ],
+        8,
+    )
+
+
+def my_half(array, core, width):
+    return lax.dynamic_slice_in_dim(array, core * width, width, axis=1)
+
+
+def all_sum(value):
+    one, two, three = (send(value, p) for p in ZS[1:])
+    value = (value + one) + (two + three)
+    value = value + send(value, FIRST)
+    return value + send(value, SECOND)
+
+
+WINDOWS = (0, 64, 192, 256)
+SCALE = HD ** (-0.5)
+
+
+def piece_copies(idx_ref, base, pieces, target, rows, sems, first_sem, cut=None):
+    copies = []
+    for number in range(32):
+        half = idx_ref[base + number]
+        row = pl.multiple_of(idx_ref[base + 32 + number], 16)
+        source = pieces[number // 4].at[number % 4]
+        if cut is not None:
+            source = source.at[:, cut]
+        copies.append(
+            pltpu.make_async_copy(
+                source, target.at[half, pl.ds(row, rows), :], sems.at[first_sem + number]
+            )
+        )
+    return copies
+
+
+def window_bias(seg_row, seg_col, b):
+    w = WINDOWS[b]
+    same = seg_col[b * 128 : (b + 1) * 128, :] == seg_row[:, w : w + 256]
+    bias = jnp.where(same, 0.0, -1e30)
+    return jnp.concatenate([bias, bias], 0)
+
+
+def two_heads(block):
+    left = lax.broadcasted_iota(jnp.int32, block.shape, 1) < HD
+    none = jnp.zeros_like(block)
+    return jnp.concatenate([jnp.where(left, block, none), jnp.where(left, none, block)], 0)
+
+
+def nt_dot(a, b):
+    return lax.dot_general(a, b, (((1,), (1,)), ((), ())), preferred_element_type=f32)
+
+
+def tn_dot(a, b):
+    return lax.dot_general(a, b, (((0,), (0,)), ((), ())), preferred_element_type=f32)
+
+
+def nn_dot(a, b):
+    return jnp.dot(a, b, preferred_element_type=f32)
+
+
+def row_norm(v):
+    center = v - jnp.mean(v, -1, keepdims=True)
+    inv = lax.rsqrt(jnp.mean(center * center, -1, keepdims=True) + norm_eps)
+    return center * inv, inv
+
+
+def attention_kernel(ready, idx_ref, seg_row_ref, seg_col_ref, *refs):
+    e_in, pieces = refs[:4], refs[4:12]
+    (e_ref, qkv_ref, lse_ref, mixed_ref, unit_ref, inv_ref, low_ref, par_ref, side_ref) = refs[12:21]
+    et_ref, w_ref, bias_ref, attended_ref, sems = refs[21:]
+    e_copies = [
+        pltpu.make_async_copy(
+            e_in[j],
+            et_ref.at[pl.ds(pl.multiple_of(idx_ref[j], 16), 192), :],
+            sems.at[j],
+        )
+        for j in range(4)
+    ]
+    w_copies = piece_copies(idx_ref, 4, pieces, w_ref, 48, sems, 4)
+    for copy in e_copies + w_copies:
+        copy.start()
+    ready()
+    for b in range(4):
+        bias_ref[b] = window_bias(seg_row_ref[...], seg_col_ref[...], b)
+    for copy in e_copies:
+        copy.wait()
+    e_ref[...] = et_ref[...].T
+    for copy in w_copies:
+        copy.wait()
+    par_ref[...] = w_ref[0, :, 1536:1664].T.astype(f32)[:8]
+    side_ref[...] = w_ref[:, :, 1536:1664]
+    for k in range(2):
+        for t in range(3):
+            part = nn_dot(e_ref[...], w_ref[k, :, t * 384 : (t + 1) * 384])
+            if t == 0:
+                part = part.astype(bf16).astype(f32) * SCALE
+            part = part.astype(bf16)
+            for i in range(3):
+                qkv_ref[t * 6 + k * 3 + i] = part[:, i * 128 : (i + 1) * 128]
+    lse_ref[...] = jnp.zeros_like(lse_ref)
+    lane = lax.broadcasted_iota(jnp.int32, (128, 128), 1)
+    left = lane < HD
+
+    @pl.loop(0, 6)
+    def _(pair):
+        for b in range(4):
+            rows = pl.ds(b * 128, 128)
+            keys = pl.ds(WINDOWS[b], 256)
+            q = qkv_ref[pair, rows, :]
+            k = qkv_ref[pair + 6, keys, :]
+            v = qkv_ref[pair + 12, keys, :]
+            s = nt_dot(two_heads(q), k) + bias_ref[b]
+            top = jnp.max(s, -1, keepdims=True)
+            e = jnp.exp(s - top)
+            total = jnp.sum(e, -1, keepdims=True)
+            log = top + jnp.log(total)
+            lse = jnp.where(lane == pair * 2, log[:128], lse_ref[rows, :])
+            lse_ref[rows, :] = jnp.where(lane == pair * 2 + 1, log[128:], lse)
+            mixed = nn_dot((e * (1.0 / total)).astype(bf16), v)
+            cols = pl.ds(pl.multiple_of(pair * 128, 128), 128)
+            mixed_ref[rows, cols] = jnp.where(left, mixed[:128], mixed[128:]).astype(bf16)
+
+    for k in range(2):
+        attended_ref[:, k * 384 : (k + 1) * 384] = nn_dot(mixed_ref[...], w_ref[k, :, 1152:1536])
+    for b in range(4):
+        rows = slice(b * 128, (b + 1) * 128)
+        unit, inv = row_norm(e_ref[rows, :].astype(f32) + attended_ref[rows, :])
+        unit_ref[rows, :] = unit
+        inv_ref[rows, :] = jnp.broadcast_to(inv, (128, 128))
+        low_ref[rows, :] = (unit * par_ref[0:1, :] + par_ref[1:2, :]).astype(bf16)
+
+
+def attention_forward(index, seg_row, seg_col, columns, pieces):
+    return staged_call(
+        attention_kernel,
+        [index],
+        [seg_row, seg_col],
+        [*columns, *pieces],
+        [
+            shaped(bf16, 512, 768),
+            shaped(bf16, 18, 512, 128),
+            shaped(f32, 512, 128),
+            shaped(bf16, 512, 768),
+            shaped(f32, 512, 768),
+            shaped(f32, 512, 128),
+            shaped(bf16, 512, 768),
+            shaped(f32, 8, 768),
+            shaped(bf16, 2, 768, 128),
+        ],
+        [
+            pltpu.VMEM((768, 512), bf16),
+            pltpu.VMEM((2, 768, 1664), bf16),
+            pltpu.VMEM((4, 256, 256), f32),
+            pltpu.VMEM((512, 768), f32),
+            pltpu.SemaphoreType.DMA((36,)),
+        ],
+        17,
+    )
+
+
+def gelu_and_slope(u):
+    square = 0.5 * u * u
+    t = 1.0 / (1.0 + (0.5 * 0.5**0.5) * jnp.abs(u))
+    poly = 0.17087277
+    for factor in (
+        -0.82215223,
+        1.48851587,
+        -1.13520398,
+        0.27886807,
+        -0.18628806,
+        0.09678418,
+        0.37409196,
+        1.00002368,
+        -1.26551223,
+    ):
+        poly = factor + t * poly
+    tail = (0.5 * t) * jnp.exp(poly - square)
+    phi = jnp.where(u < 0, tail, 1.0 - tail)
+    return u * phi, phi + (u * 0.3989422804014327) * jnp.exp(-square)
+
+
+def up_kernel(ready, idx_ref, low_ref, *refs):
+    pieces, act_ref, slope_ref, w_ref, sems = refs[:8], refs[8], refs[9], refs[10], refs[11]
+    copies = piece_copies(idx_ref, 0, pieces, w_ref, 48, sems, 0)
+    for copy in copies:
+        copy.start()
+    ready()
+    for copy in copies:
+        copy.wait()
+    for k in range(2):
+
+        @pl.loop(0, 6)
+        def _(n):
+            cols = pl.ds(pl.multiple_of(n * 256, 256), 256)
+            u = nn_dot(low_ref[...], w_ref[k, :, cols])
+            value, slope = gelu_and_slope(u)
+            out_cols = pl.ds(pl.multiple_of(k * 1536 + n * 256, 256), 256)
+            act_ref[:, out_cols] = value.astype(bf16)
+            slope_ref[:, out_cols] = slope.astype(bf16)
+
+
+def up_forward(index, low, pieces):
+    return staged_call(
+        up_kernel,
+        [index],
+        [low],
+        pieces,
+        [
+            shaped(bf16, 512, 3072),
+            shaped(bf16, 512, 3072),
+        ],
+        [
+            pltpu.VMEM((2, 768, 1536), bf16),
+            pltpu.SemaphoreType.DMA((32,)),
+        ],
+        18,
+    )
+
+
+def thirds(v):
+    high = v.astype(bf16)
+    rest = v - high.astype(f32)
+    middle = rest.astype(bf16)
+    return high, middle, (rest - middle.astype(f32)).astype(bf16)
+
+
+def half_copies(core, own, other, target, sems):
+    return [
+        pltpu.make_async_copy(own, target.at[core], sems.at[0]),
+        pltpu.make_async_copy(other, target.at[1 - core], sems.at[1]),
+    ]
+
+
+def down_kernel(ready, idx_ref, seg_row_ref, act_ref, unit_one_ref, par_ref, *refs):
+    unit_ref, inv_ref, frag_ref, frag_low_ref, size_ref, w_ref, result_ref, sems = refs[2:]
+    copies = half_copies(idx_ref[0], refs[0], refs[1], w_ref, sems)
+    for copy in copies:
+        copy.start()
+    ready()
+    for copy in copies:
+        copy.wait()
+    for k in range(2):
+        result_ref[:, k * 384 : (k + 1) * 384] = nn_dot(act_ref[...], w_ref[k])
+    pooled = jnp.zeros((32, 768), f32)
+    for b in range(4):
+        rows = slice(b * 128, (b + 1) * 128)
+        one = unit_one_ref[rows, :] * par_ref[0:1, :] + par_ref[1:2, :]
+        unit, inv = row_norm(one + result_ref[rows, :])
+        unit_ref[rows, :] = unit
+        inv_ref[rows, :] = jnp.broadcast_to(inv, (128, 128))
+        two = unit * par_ref[2:3, :] + par_ref[3:4, :]
+        member = lax.broadcasted_iota(jnp.int32, (32, 128), 0) == seg_row_ref[:, rows]
+        member = jnp.where(member, 1.0, 0.0).astype(bf16)
+        for part in thirds(two):
+            pooled += nn_dot(member, part)
+    size = lax.rsqrt(jnp.sum(pooled * pooled, -1, keepdims=True) + unit_eps)
+    frag = pooled * size
+    frag_ref[...] = frag
+    frag_low_ref[...] = frag.astype(bf16)
+    size_ref[...] = jnp.broadcast_to(size, (32, 128))
+
+
+def down_forward(index, seg_row, act, unit_one, params, pieces):
+    return staged_call(
+        down_kernel,
+        [index],
+        [seg_row, act, unit_one, params],
+        pieces,
+        [
+            shaped(f32, 512, 768),
+            shaped(f32, 512, 128),
+            shaped(f32, 32, 768),
+            shaped(bf16, 32, 768),
+            shaped(f32, 32, 128),
+        ],
+        [
+            pltpu.VMEM((2, 3072, 384), bf16),
+            pltpu.VMEM((512, 768), f32),
+            pltpu.SemaphoreType.DMA((2,)),
+        ],
+        10,
+    )
+
+
+def back_norm(upstream, unit, inv, gain):
+    scaled = upstream * gain
+    return inv * (
+        scaled
+        - jnp.mean(scaled, -1, keepdims=True)
+        - unit * jnp.mean(scaled * unit, -1, keepdims=True)
+    )
+
+
+def loss_kernel(
+    ready, idx_ref, heat_ref, seg_col_ref, partner_ref, own_weight_ref, partner_row_ref, side_ref,
+    frag_ref, size_ref, unit_ref, inv_ref, par_ref, slope_ref, *refs
+):
+    blocks, down_pieces = refs[:8], refs[8:10]
+    loss_ref, low_own_ref, low_other_ref, gup_own_ref, gup_other_ref, two_ref, gains_ref = refs[10:17]
+    all_ref, down_ref, low_ref, spread_ref, sems, w_sems = refs[17:]
+    copies = []
+    for number in range(32):
+        row = pl.multiple_of(idx_ref[1 + number], 16)
+        copies.append(
+            pltpu.make_async_copy(
+                blocks[number // 4].at[number % 4], all_ref.at[pl.ds(row, 32), :], sems.at[number]
+            )
+        )
+    core = idx_ref[33]
+    down_copies = half_copies(core, down_pieces[0], down_pieces[1], down_ref, w_sems)
+    for copy in copies + down_copies:
+        copy.start()
+    ready()
+    for copy in copies:
+        copy.wait()
+    base = idx_ref[0]
+    inv_heat = 1.0 / heat_ref[0]
+    tally = 1024
+    mine = all_ref[pl.ds(pl.multiple_of(base, 16), 32), :]
+    grid = (nt_dot(mine, all_ref[...]) - 1.0) * inv_heat
+    across = lax.broadcasted_iota(jnp.int32, (32, tally), 1)
+    down = lax.broadcasted_iota(jnp.int32, (32, tally), 0) + base
+    powers = jnp.where(across == down, 0.0, jnp.exp(grid))
+    total = jnp.sum(powers, -1, keepdims=True)
+    chosen = across == partner_ref[...]
+    target = jnp.sum(jnp.where(chosen, grid, 0.0), -1, keepdims=True)
+    terms = own_weight_ref[...] * (jnp.log(total) - target)
+    loss_ref[...] = jnp.broadcast_to(jnp.sum(terms, 0, keepdims=True) / tally, (8, 128))
+    pull = powers / total - jnp.where(chosen, 1.0, 0.0)
+    pull = (pull * (own_weight_ref[...] * (inv_heat / tally))).astype(bf16)
+    grad = nn_dot(pull, all_ref[...])
+    for big in range(2):
+        many = all_ref[big * 512 : (big + 1) * 512, :]
+        spread_ref[...] = nt_dot(many, all_ref[...])
+        close = nt_dot(many, mine)
+        parts = []
+        for b in range(big * 4, big * 4 + 4):
+            inside = slice((b - big * 4) * 128, (b - big * 4 + 1) * 128)
+            spread = jnp.exp((spread_ref[inside, :] - 1.0) * inv_heat)
+            number = lax.broadcasted_iota(jnp.int32, (128, 128), 0)
+            same = number == lax.broadcasted_iota(jnp.int32, (128, 128), 1)
+            spread_total = sum(
+                jnp.where(same, 0.0, spread[:, n * 128 : (n + 1) * 128])
+                if n == b
+                else spread[:, n * 128 : (n + 1) * 128]
+                for n in range(8)
+            )
+            spread_total = jnp.sum(spread_total, -1, keepdims=True)
+            part = jnp.exp((close[inside, :] - 1.0) * inv_heat)
+            here = lax.broadcasted_iota(jnp.int32, (128, 32), 0) + b * 128
+            column = lax.broadcasted_iota(jnp.int32, (128, 32), 1) + base
+            part = jnp.where(here == column, 0.0, part) / spread_total
+            part = part - jnp.where(here == partner_row_ref[...], 1.0, 0.0)
+            side = jnp.concatenate(
+                [
+                    side_ref[n % 2, (n // 2) * 48 : (n // 2) * 48 + 32, :].astype(f32)
+                    for n in range(b * 4, b * 4 + 4)
+                ],
+                0,
+            )
+            lanes = lax.broadcasted_iota(jnp.int32, (128, 128), 1)
+            wanted = jnp.logical_and(lanes >= 4, lanes < 7)
+            weight = jnp.sum(jnp.where(wanted, side, 0.0), -1, keepdims=True)
+            parts.append((part * (weight * (inv_heat / tally))).astype(bf16))
+        grad += tn_dot(jnp.concatenate(parts, 0), many)
+    frag = frag_ref[...]
+    pooled = size_ref[:, 0:1] * (grad - frag * jnp.sum(grad * frag, -1, keepdims=True))
+    stacked = jnp.concatenate(thirds(pooled), 0)
+    gain_two = jnp.zeros((1, 768), f32)
+    shift_two = jnp.zeros((1, 768), f32)
+    for b in range(4):
+        rows = slice(b * 128, (b + 1) * 128)
+        slot = lax.broadcasted_iota(jnp.int32, (128, 96), 1) % 32
+        member = jnp.where(slot == seg_col_ref[rows, :], 1.0, 0.0).astype(bf16)
+        upstream = nn_dot(member, stacked)
+        unit = unit_ref[rows, :]
+        back = back_norm(upstream, unit, inv_ref[rows, 0:1], par_ref[2:3, :])
+        two_ref[rows, :] = back
+        low_ref[rows, :] = back.astype(bf16)
+        gain_two += jnp.sum(upstream * unit, 0, keepdims=True)
+        shift_two += jnp.sum(upstream, 0, keepdims=True)
+    halves = (core, 1 - core)
+    for half, ref in zip(halves, (low_own_ref, low_other_ref)):
+        ref[...] = low_ref[:, pl.ds(pl.multiple_of(half * 384, 128), 384)]
+    for copy in down_copies:
+        copy.wait()
+    for half, gup_ref in zip(halves, (gup_own_ref, gup_other_ref)):
+
+        @pl.loop(0, 6)
+        def _(n):
+            cols = pl.ds(pl.multiple_of(n * 256, 256), 256)
+            wide = pl.ds(pl.multiple_of(half * 1536 + n * 256, 256), 256)
+            g = sum(
+                nt_dot(low_ref[:, k * 384 : (k + 1) * 384], down_ref[k, wide, :])
+                for k in range(2)
+            )
+            gup_ref[:, cols] = (g * slope_ref[:, wide].astype(f32)).astype(bf16)
+
+    gains_ref[...] = jnp.concatenate([gain_two, shift_two, jnp.zeros((6, 768), f32)], 0)
+
+
+def loss_backward(index, heat, arrays, pieces):
+    return staged_call(
+        loss_kernel,
+        [index, heat],
+        arrays,
+        pieces,
+        [
+            shaped(f32, 8, 128),
+            shaped(bf16, 512, 384),
+            shaped(bf16, 512, 384),
+            shaped(bf16, 512, 1536),
+            shaped(bf16, 512, 1536),
+            shaped(f32, 512, 768),
+            shaped(f32, 8, 768),
+        ],
+        [
+            pltpu.VMEM((1024, 768), bf16),
+            pltpu.VMEM((2, 3072, 384), bf16),
+            pltpu.VMEM((512, 768), bf16),
+            pltpu.VMEM((512, 1024), f32),
+            pltpu.SemaphoreType.DMA((32,)),
+            pltpu.SemaphoreType.DMA((2,)),
+        ],
+        18,
+    )
+
+
+def ffn_back_kernel(
+    ready, idx_ref, gup_own_ref, gup_other_ref, two_ref, unit_ref, inv_ref, par_ref, *refs
+):
+    pieces = refs[:8]
+    resid_ref, att_ref, own_ref, other_ref, gains_ref, up_ref, sems = refs[8:]
+    copies = piece_copies(idx_ref, 0, pieces, up_ref, 48, sems, 0)
+    for copy in copies:
+        copy.start()
+    ready()
+    for copy in copies:
+        copy.wait()
+    core = idx_ref[0]
+    for n in range(3):
+        cols = slice(n * 256, (n + 1) * 256)
+        resid_ref[:, cols] = (
+            two_ref[:, cols]
+            + nt_dot(gup_own_ref[...], up_ref[core, cols, :])
+            + nt_dot(gup_other_ref[...], up_ref[1 - core, cols, :])
+        )
+    gain_sum = jnp.zeros((1, 768), f32)
+    shift_sum = jnp.zeros((1, 768), f32)
+    for b in range(4):
+        rows = slice(b * 128, (b + 1) * 128)
+        one = resid_ref[rows, :]
+        unit = unit_ref[rows, :]
+        back = back_norm(one, unit, inv_ref[rows, 0:1], par_ref[0:1, :])
+        resid_ref[rows, :] = back
+        att_ref[rows, :] = back.astype(bf16)
+        gain_sum += jnp.sum(one * unit, 0, keepdims=True)
+        shift_sum += jnp.sum(one, 0, keepdims=True)
+    for half, ref in ((core, own_ref), (1 - core, other_ref)):
+        ref[...] = att_ref[:, pl.ds(pl.multiple_of(half * 384, 128), 384)]
+    gains_ref[...] = jnp.concatenate([gain_sum, shift_sum, jnp.zeros((6, 768), f32)], 0)
+
+
+def ffn_backward(index, arrays, pieces):
+    return staged_call(
+        ffn_back_kernel,
+        [index],
+        arrays,
+        pieces,
+        [
+            shaped(f32, 512, 768),
+            shaped(bf16, 512, 768),
+            shaped(bf16, 512, 384),
+            shaped(bf16, 512, 384),
+            shaped(f32, 8, 768),
+        ],
+        [pltpu.VMEM((2, 768, 1536), bf16), pltpu.SemaphoreType.DMA((32,))],
+        9,
+    )
+
+
+def heads_back(half, gm_ref, qkv_ref, lse_ref, bias_ref, gqkv_ref, gk_ref, gv_ref):
+    lane = lax.broadcasted_iota(jnp.int32, (128, 128), 1)
+    left = lane < HD
+    gk_ref[...] = jnp.zeros_like(gk_ref)
+    gv_ref[...] = jnp.zeros_like(gv_ref)
+
+    @pl.loop(0, 3)
+    def _(spot):
+        pair = half * 3 + spot
+        for b in range(4):
+            rows = pl.ds(b * 128, 128)
+            keys = pl.ds(WINDOWS[b], 256)
+            q = qkv_ref[pair, rows, :]
+            k = qkv_ref[pair + 6, keys, :]
+            v = qkv_ref[pair + 12, keys, :]
+            gm = gm_ref[rows, pl.ds(pl.multiple_of(spot * 128, 128), 128)]
+            q, gm = two_heads(q), two_heads(gm)
+            stats = lse_ref[rows, :]
+            lse = jnp.concatenate(
+                [
+                    jnp.sum(jnp.where(lane == pair * 2 + h, stats, 0.0), -1, keepdims=True)
+                    for h in range(2)
+                ],
+                0,
+            )
+            p = jnp.exp(nt_dot(q, k) + bias_ref[b] - lse)
+            gp = nt_dot(gm, v)
+            gs = (p * (gp - jnp.sum(gp * p, -1, keepdims=True))).astype(bf16)
+            gq = nn_dot(gs, k)
+            gq = (jnp.where(left, gq[:128], gq[128:]) * SCALE).astype(bf16)
+            gqkv_ref[rows, pl.ds(pl.multiple_of(spot * 128, 128), 128)] = gq
+            gk_ref[spot, keys, :] += tn_dot(gs, q)
+            gv_ref[spot, keys, :] += tn_dot(p.astype(bf16), gm)
+        for third, ref in ((1, gk_ref), (2, gv_ref)):
+            cols = pl.ds(pl.multiple_of(third * 384 + spot * 128, 128), 128)
+            gqkv_ref[:, cols] = ref[spot].astype(bf16)
+
+
+def other_heads_kernel(ready, idx_ref, seg_row_ref, seg_col_ref, qkv_ref, lse_ref, att_ref, resid_ref, *refs
+):
+    pieces = refs[:8]
+    gqkv_ref, gm_own_ref, part_ref = refs[8:11]
+    w_ref, bias_ref, gm_ref, gk_ref, gv_ref, sems = refs[11:]
+    copies = piece_copies(idx_ref, 4, pieces, w_ref, 48, sems, 0)
+    for copy in copies:
+        copy.start()
+    ready()
+    for b in range(4):
+        bias_ref[b] = window_bias(seg_row_ref[...], seg_col_ref[...], b)
+    for copy in copies:
+        copy.wait()
+    core = idx_ref[4]
+    half = 1 - core
+    for side, ref in ((half, gm_ref), (core, gm_own_ref)):
+        rows = pl.ds(pl.multiple_of(side * 384, 128), 384)
+        ref[...] = sum(
+            nt_dot(att_ref[:, k * 384 : (k + 1) * 384], w_ref[k, rows, 1152:1536])
+            for k in range(2)
+        ).astype(bf16)
+    heads_back(half, gm_ref, qkv_ref, lse_ref, bias_ref, gqkv_ref, gk_ref, gv_ref)
+    for n in range(3):
+        cols = slice(n * 256, (n + 1) * 256)
+        part_ref[:, cols] = resid_ref[:, cols] + nt_dot(gqkv_ref[...], w_ref[half, cols, :1152])
+
+
+def other_heads(index, arrays, pieces):
+    return staged_call(
+        other_heads_kernel,
+        [index],
+        arrays,
+        pieces,
+        [
+            shaped(bf16, 512, 1152),
+            shaped(bf16, 512, 384),
+            shaped(f32, 512, 768),
+        ],
+        [
+            pltpu.VMEM((2, 768, 1664), bf16),
+            pltpu.VMEM((4, 256, 256), f32),
+            pltpu.VMEM((512, 384), bf16),
+            pltpu.VMEM((3, 512, 128), f32),
+            pltpu.VMEM((3, 512, 128), f32),
+            pltpu.SemaphoreType.DMA((32,)),
+        ],
+        17,
+    )
+
+
+def own_heads_kernel(ready, idx_ref, seg_row_ref, seg_col_ref, qkv_ref, lse_ref, gm_ref, part_ref, *refs
+):
+    pieces = refs[:4]
+    gqkv_ref, outs = refs[4], refs[5:9]
+    w_ref, bias_ref, gk_ref, gv_ref, et_ref, sems = refs[9:]
+    copies = []
+    for number in range(16):
+        row = pl.multiple_of(idx_ref[36 + number], 16)
+        copies.append(
+            pltpu.make_async_copy(
+                pieces[number // 4].at[number % 4], w_ref.at[pl.ds(row, 48), :], sems.at[number]
+            )
+        )
+    for copy in copies:
+        copy.start()
+    ready()
+    for b in range(4):
+        bias_ref[b] = window_bias(seg_row_ref[...], seg_col_ref[...], b)
+    core = idx_ref[4]
+    heads_back(core, gm_ref, qkv_ref, lse_ref, bias_ref, gqkv_ref, gk_ref, gv_ref)
+    for copy in copies:
+        copy.wait()
+    for n in range(3):
+        cols = slice(n * 256, (n + 1) * 256)
+        total = part_ref[:, cols] + nt_dot(gqkv_ref[...], w_ref[cols, :1152])
+        et_ref[cols, :] = total.astype(bf16).T
+    for j in range(4):
+        outs[j][...] = et_ref[pl.ds(pl.multiple_of(idx_ref[j], 16), 192), :]
+
+
+def own_heads(index, arrays, pieces):
+    return staged_call(
+        own_heads_kernel,
+        [index],
+        arrays,
+        pieces,
+        [
+            shaped(bf16, 512, 1152),
+            shaped(bf16, 192, 512),
+            shaped(bf16, 192, 512),
+            shaped(bf16, 192, 512),
+            shaped(bf16, 192, 512),
+        ],
+        [
+            pltpu.VMEM((768, 1664), bf16),
+            pltpu.VMEM((4, 256, 256), f32),
+            pltpu.VMEM((3, 512, 128), f32),
+            pltpu.VMEM((3, 512, 128), f32),
+            pltpu.VMEM((768, 512), bf16),
+            pltpu.SemaphoreType.DMA((16,)),
+        ],
+        15,
+    )
+
+
+def to_slots(idx_ref, whole_ref, keep_ref, away_ref):
+    for slot in range(8):
+        keep_ref[slot] = whole_ref[idx_ref[slot]]
+        away_ref[slot] = whole_ref[idx_ref[8 + slot]]
+
+
+def down_grad_kernel(ready, idx_ref, act_ref, act_o_ref, g_ref, g_o_ref, keep_ref, away_ref, whole_ref):
+    ready()
+    for n in range(8):
+        cols = slice(n * 384, (n + 1) * 384)
+        total = tn_dot(act_ref[:, cols], g_ref[...]) + tn_dot(act_o_ref[:, cols], g_o_ref[...])
+        total = total.astype(bf16)
+        whole_ref[2 * n] = total[:192]
+        whole_ref[2 * n + 1] = total[192:]
+    to_slots(idx_ref, whole_ref, keep_ref, away_ref)
+
+
+def down_grad(index, arrays):
+    return staged_call(
+        down_grad_kernel,
+        [index],
+        arrays,
+        [],
+        [shaped(bf16, 8, 192, 384)] * 2,
+        [pltpu.VMEM((16, 192, 384), bf16)],
+        7,
+    )
+
+
+def store_chunks(whole_ref, cols, total):
+    for f in range(16):
+        whole_ref[f, :, cols] = total[f * 48 : (f + 1) * 48]
+
+
+def up_out_grad_kernel(
+    ready, idx_ref, low_ref, low_o_ref, g_ref, g_o_ref, mixed_ref, mixed_o_ref, ga_ref, ga_o_ref, norms_ref,
+    keep_ref, away_ref, whole_ref, t_ref,
+):
+    ready()
+    t_ref[0] = low_ref[...].T
+    t_ref[1] = low_o_ref[...].T
+    for n in range(3):
+        cols = slice(n * 512, (n + 1) * 512)
+        total = nn_dot(t_ref[0], g_ref[:, cols]) + nn_dot(t_ref[1], g_o_ref[:, cols])
+        store_chunks(whole_ref, cols, total.astype(bf16))
+    t_ref[0] = mixed_ref[...].T
+    t_ref[1] = mixed_o_ref[...].T
+    total = nn_dot(t_ref[0], ga_ref[...]) + nn_dot(t_ref[1], ga_o_ref[...])
+    store_chunks(whole_ref, slice(1536, 1920), total.astype(bf16))
+    norms = norms_ref[...].T.astype(bf16)
+    norms = jnp.concatenate([norms, jnp.zeros((768, 120), bf16)], 1)
+    store_chunks(whole_ref, slice(1920, 2048), norms)
+    to_slots(idx_ref, whole_ref, keep_ref, away_ref)
+
+
+def up_out_grad(index, arrays):
+    return staged_call(
+        up_out_grad_kernel,
+        [index],
+        arrays,
+        [],
+        [
+            shaped(bf16, 8, 48, 2048),
+            shaped(bf16, 8, 48, 2048),
+        ],
+        [
+            pltpu.VMEM((16, 48, 2048), bf16),
+            pltpu.VMEM((2, 768, 512), bf16),
+        ],
+        8,
+    )
+
+
+def in_grad_kernel(ready, idx_ref, e_ref, e_o_ref, g_ref, g_o_ref, keep_ref, away_ref, whole_ref, t_ref):
+    ready()
+    t_ref[0] = e_ref[...].T
+    t_ref[1] = e_o_ref[...].T
+    for t in range(3):
+        cols = slice(t * 384, (t + 1) * 384)
+        total = nn_dot(t_ref[0], g_ref[:, cols]) + nn_dot(t_ref[1], g_o_ref[:, cols])
+        store_chunks(whole_ref, cols, total.astype(bf16))
+    to_slots(idx_ref, whole_ref, keep_ref, away_ref)
+
+
+def in_grad(index, arrays):
+    return staged_call(
+        in_grad_kernel,
+        [index],
+        arrays,
+        [],
+        [
+            shaped(bf16, 8, 48, 1152),
+            shaped(bf16, 8, 48, 1152),
+        ],
+        [
+            pltpu.VMEM((16, 48, 1152), bf16),
+            pltpu.VMEM((2, 768, 512), bf16),
+        ],
+        6,
+    )
+
+
+def optimizer_kernel(ready, core_ref, fix_ref, totals_ref, totals_o_ref, *refs):
+    ready()
+    own, other = refs[:4], refs[4:8]
+    params, outs = refs[8:26], refs[26:46]
+    table_ref = refs[46]
+    core = core_ref[0]
+    totals = totals_ref[...] + totals_o_ref[...]
+    norm = jnp.sqrt(totals[:, 0:1])
+    outs[0][...] = totals[:, 1:2]
+    outs[1][...] = norm
+    factor = clip_norm / jnp.maximum(norm, clip_norm)
+    fix_one, fix_two = 1.0 / fix_ref[0], 1.0 / fix_ref[1]
+
+    def update(number, spot, grad, rate, decay):
+        w_ref, first_ref, second_ref = params[3 * number : 3 * number + 3]
+        grad = grad.astype(f32) * factor
+        weight = w_ref[spot]
+        first = beta_one * first_ref[spot] + (1.0 - beta_one) * grad
+        second = beta_two * second_ref[spot] + (1.0 - beta_two) * grad * grad
+        step = (first * fix_one) / (jnp.sqrt(second * fix_two) + adam_eps)
+        outs[2 + 3 * number][spot] = weight - rate * (step + decay * weight)
+        outs[3 + 3 * number][spot] = first
+        outs[4 + 3 * number][spot] = second
+
+    every = slice(None)
+    for side, (table, into, up_out, down) in enumerate((own, other)):
+        half = core if side == 0 else 1 - core
+
+        def columns(width, start=0):
+            return pl.ds(pl.multiple_of(half * width + start, 128), width)
+
+        table_ref[:, columns(VOCAB_HALF)] = table[...]
+        for t in range(3):
+            update(
+                1,
+                (every, columns(384, t * 768)),
+                into[:, t * 384 : (t + 1) * 384],
+                rate_matrix,
+                decay_rate,
+            )
+        update(2, (every, columns(384)), up_out[:, 1536:1920], rate_matrix, decay_rate)
+        for t in range(3):
+            spot = pl.ds(pl.multiple_of(half * 1536 + t * 512, 128), 512)
+            update(3, (every, spot), up_out[:, t * 512 : (t + 1) * 512], rate_matrix, decay_rate)
+        for t in range(4):
+            rows = slice(t * 48, (t + 1) * 48)
+            update(4, (rows, columns(384)), down[rows, :], rate_matrix, decay_rate)
+    vocab = params[0].shape[1]
+    for low in range(0, vocab, 512):
+        spot = slice(low, min(vocab, low + 512))
+        update(0, (every, spot), table_ref[:, spot], rate_embed, decay_rate)
+    norms = jnp.where(core == 0, own[2][:, 1920:].astype(f32), other[2][:, 1920:].astype(f32))
+    update(5, (every, every), norms.T[:4], rate_norm, 0.0)
+
+
+def optimizer(core, fixes, totals, totals_o, own, other, params):
+    return staged_call(
+        optimizer_kernel,
+        [core, fixes],
+        [totals, totals_o, *own, *other, *params],
+        [],
+        [
+            shaped(f32, 1, 1),
+            shaped(f32, 1, 1),
+            *[shaped(f32, *p.shape) for p in params],
+        ],
+        [
+            pltpu.VMEM((48, VOCAB_PAD), bf16),
+        ],
+        8,
+    )
+
+
+def per_device_links(
+    kmer_identifiers,
+    slot_fragment_ids,
+    mirror_fragment_index,
+    fragment_weight,
+    affinity_heat,
+    optimizer_iteration,
+    lexicon_table,
+    lexicon_first_moment,
+    lexicon_raw_moment,
+    query_key_value_maps,
+    qkv_first_moment,
+    qkv_raw_moment,
+    attention_exit_map,
+    exit_first_moment,
+    exit_raw_moment,
+    widening_matrix_in,
+    widening_first_moment,
+    widening_raw_moment,
+    narrowing_matrix_out,
+    narrowing_first_moment,
+    narrowing_raw_moment,
+    layernorm_scale_bias,
+    layernorm_first_moment,
+    layernorm_raw_moment,
+):
+    place = Place()
+    core = place.core
+    vocab = lexicon_table.shape[0]
+    table_cut = jnp.pad(lexicon_table.T.astype(bf16), ((0, 0), (0, VOCAB_PAD - vocab)))
+    table_half = my_half(table_cut, core, VOCAB_HALF)
+    near = [send(table_half, FIRST), send(table_half, SECOND)]
+    near.append(send(near[0], SECOND))
+    ids_z = jnp.stack(
+        [kmer_identifiers] + [send(kmer_identifiers, ZS[j]) for j in (1, 2, 3)]
+    )
+    others = send(after(jnp.stack(near), ids_z), CORE)
+    norm_cut = layernorm_scale_bias.T.astype(bf16)
+    heavy = jnp.stack(thirds(fragment_weight), 1)
+    extra = jnp.concatenate(
+        [
+            norm_cut,
+            jnp.pad(heavy, ((0, 16), (0, 0))),
+            jnp.zeros((48, 121), bf16),
+        ],
+        1,
+    )
+    low_in = query_key_value_maps.astype(bf16)
+    low_out = attention_exit_map.astype(bf16)
+    low_up = widening_matrix_in.astype(bf16)
+    low_down = narrowing_matrix_out.astype(bf16)
+    in_out_cut = jnp.concatenate(
+        [my_half(low_in[:, k * 768 : (k + 1) * 768], core, 384) for k in range(3)]
+        + [my_half(low_out, core, 384), extra],
+        1,
+    )
+    both_cut = jnp.concatenate([in_out_cut, my_half(low_up, core, 1536)], 1)
+    both_far = z_sends(after(both_cut, table_half))
+    down_half = my_half(low_down, core, 384)
+    down_own = lax.all_gather(after(down_half, *near), "fsdp", axis=0, tiled=True)
+    slots = [place.y * 2 + place.x]
+    for side in (core, 1 - core):
+        slots += [place.plane_slot(side, a, b) for a, b in ((1, 0), (0, 1), (1, 1))]
+    index = jnp.stack(
+        [s * 48 for s in slots] + [core * VOCAB_HALF, (1 - core) * VOCAB_HALF]
+    ).astype(jnp.int32)
+    found = lookup(index, ids_z, [table_cut] + near + [others])
+    both_far = together(both_far, *found)
+    in_out_column = jnp.stack([p[:, :1664] for p in both_far])
+    up_column = jnp.stack([p[:, 1664:] for p in both_far])
+    columns = [found[0]] + [send(found[j], ZS[j]) for j in (1, 2, 3)]
+    in_out_mine = plane_sends(in_out_column, False, columns)
+    in_out = both_cores(together(in_out_mine, in_out_mine[3]))
+    up_mine = plane_sends(after(up_column, in_out_mine[3]), True)
+    seg_row = slot_fragment_ids
+    seg_col = slot_fragment_ids.reshape(512, 1)
+    index_48 = piece_index(place, 48)
+    z_index = jnp.stack([(place.z ^ j) * 192 for j in range(4)]).astype(jnp.int32)
+    attention_index = jnp.concatenate([z_index, index_48])
+    embedded, qkv, lse, mixed, unit_one, inv_one, normed_low, params, side = attention_forward(
+        attention_index, seg_row, seg_col, columns, in_out
+    )
+    up_w = both_cores(together(up_mine, normed_low))
+    activated, slope = up_forward(index_48, normed_low, up_w)
+    down_w = [down_own, send(after(down_own, normed_low), CORE)]
+    core_index = core.astype(jnp.int32).reshape(1)
+    unit_two, inv_two, unit_rows, unit_low, unit_scale = down_forward(
+        core_index, seg_row, activated, unit_one, params, down_w
+    )
+    embedded_o, mixed_o, normed_o, activated_o = (
+        send(a, CORE) for a in (embedded, mixed, normed_low, activated)
+    )
+    column = jnp.stack([unit_low] + [send(unit_low, ZS[j]) for j in (1, 2, 3)])
+    blocks = [column, send(column, FIRST), send(column, SECOND), send(column, BOTH)]
+    blocks = blocks + [send(block, CORE) for block in blocks]
+    base = (lax.axis_index("fsdp") * 2 + core) * 32
+    index = [base]
+    for who in (core, 1 - core):
+        for a, b in ((0, 0), (1, 0), (0, 1), (1, 1)):
+            index += [(place.chip(who, j, a, b) * 2 + who) * 32 for j in range(4)]
+    index += [core]
+    (
+        loss_tile, grad_result_own, grad_result_x, grad_up_own, grad_up_x, grad_two, gains_two,
+    ) = loss_backward(
+        jnp.stack(index).astype(jnp.int32),
+        affinity_heat.reshape(1),
+        [
+            seg_col,
+            mirror_fragment_index.reshape(32, 1),
+            fragment_weight.reshape(32, 1),
+            mirror_fragment_index.reshape(1, 32),
+            side,
+            unit_rows,
+            unit_scale,
+            unit_two,
+            inv_two,
+            params,
+            slope,
+        ],
+        blocks + down_w,
+    )
+    slots = slot_index(place)
+    grad_result_o = send(grad_result_x, CORE)
+    ids_o = send(ids_z, CORE)
+    grad_up_o = send(grad_up_x, CORE)
+    spare = [embedded_o, mixed_o, normed_o, ids_o]
+    down_keep, down_away = down_grad(
+        slots, [after(activated, *spare), activated_o, grad_result_own, grad_result_o]
+    )
+    down_came = send(down_away, SECOND)
+    grad_resid, grad_attended, grad_att_own, grad_att_x, gains_one = ffn_backward(
+        index_48,
+        [after(grad_up_own, down_away), grad_up_x, grad_two, unit_one, inv_one, params],
+        up_w,
+    )
+    grad_att_o = send(grad_att_x, CORE)
+    norms = jnp.concatenate([gains_one[:2], gains_two[:2], jnp.zeros((4, 768), f32)], 0)
+    norms = norms + send(norms, CORE)
+    up_out_keep, up_out_away = up_out_grad(
+        slots,
+        [
+            normed_low,
+            normed_o,
+            grad_up_own,
+            grad_up_o,
+            mixed,
+            mixed_o,
+            grad_att_own,
+            grad_att_o,
+            norms,
+        ],
+    )
+    up_out_came = send(up_out_away, SECOND)
+    down_came = after(down_came, up_out_away)
+    down_across = scatter_add(down_keep, down_came)
+    down_came_two = send(down_across, FIRST)
+    grad_qkv_x, grad_mixed_own, part = other_heads(
+        attention_index,
+        [seg_row, seg_col, qkv, lse, after(grad_attended, down_across), grad_resid],
+        in_out,
+    )
+    grad_qkv_o = send(grad_qkv_x, CORE)
+    down_came_two, up_out_came = together([down_came_two, up_out_came], part)
+    down_here, down_far = scatter_here(down_keep, down_came, down_came_two)
+    up_out_across = scatter_add(up_out_keep, up_out_came)
+    up_out_came_two = send(up_out_across, FIRST)
+    down_far_came = line_sends(down_far)
+    grad_qkv_own, *outs = own_heads(
+        attention_index,
+        [seg_row, seg_col, qkv, lse, grad_mixed_own, after(part, up_out_across, *down_far)],
+        in_out[:4],
+    )
+    far_cols = [send(outs[j], ZS[j]) for j in (1, 2, 3)]
+    *down_far_came, up_out_came_two, grad_qkv_o = together(
+        down_far_came + [up_out_came_two, grad_qkv_o], grad_qkv_own
+    )
+    down_sum = line_sum(down_here, down_far_came)
+    in_keep, in_away = in_grad(slots, [embedded, embedded_o, grad_qkv_own, grad_qkv_o])
+    far_cols = together(far_cols, in_away)
+    in_came = send(after(in_away, *far_cols), SECOND)
+    token_cols = jnp.stack([outs[0]] + far_cols)
+    token_cols_o = send(token_cols, CORE)
+    up_out_here, up_out_far = scatter_here(
+        up_out_keep, up_out_came, after(up_out_came_two, token_cols)
+    )
+    up_out_far_came = line_sends(up_out_far)
+    plane = [place.plane_slot(core, a, b) * 48 for a, b in ((0, 0), (1, 0), (0, 1), (1, 1))]
+    keep, away = token_sum(
+        jnp.stack([core * VOCAB_HALF] + plane).astype(jnp.int32),
+        after(ids_z, *up_out_far),
+        ids_o,
+        token_cols,
+        token_cols_o,
+    )
+    came = send(away, SECOND)
+    in_came = after(in_came, away)
+    in_across = scatter_add(in_keep, in_came)
+    in_came_two = send(in_across, FIRST)
+    across = (keep[1].astype(f32) + came[1].astype(f32)).astype(bf16)
+    came_two = send(across, FIRST)
+    in_here, in_far = scatter_here(in_keep, in_came, after(in_came_two, across))
+    in_far_came = line_sends(in_far)
+    up_out_sum = line_sum(up_out_here, together(up_out_far_came, across))
+    table_sum = keep[0].astype(f32) + came[0].astype(f32) + came_two.astype(f32)
+    table_sum = table_sum.astype(bf16)
+    in_sum = line_sum(in_here, together(in_far_came, table_sum))
+    sums = [table_sum, in_sum, up_out_sum, down_sum]
+    sums_o = [send(s, CORE) for s in sums]
+    squares = sum(
+        jnp.sum(jnp.square(p.astype(f32)))
+        for p in (sums[0], sums[1], sums[2][:, :1920], sums[3])
+    )
+    norm_own = sums[2][:, 1920:1924].astype(f32)
+    squares += jnp.where(core == 0, jnp.sum(norm_own * norm_own), 0.0)
+    totals = jnp.concatenate([squares.reshape(1, 1), loss_tile[:1, :1]], 1)
+    totals = all_sum(after(totals, *sums_o))
+    count_now = optimizer_iteration.astype(f32)
+    fixes = jnp.stack([1.0 - jnp.power(beta_one, count_now), 1.0 - jnp.power(beta_two, count_now)])
+    results = optimizer(
+        core_index,
+        fixes,
+        totals,
+        send(totals, CORE),
+        sums,
+        sums_o,
+        [
+            lexicon_table.T,
+            lexicon_first_moment.T,
+            lexicon_raw_moment.T,
+            query_key_value_maps,
+            qkv_first_moment,
+            qkv_raw_moment,
+            attention_exit_map,
+            exit_first_moment,
+            exit_raw_moment,
+            widening_matrix_in,
+            widening_first_moment,
+            widening_raw_moment,
+            narrowing_matrix_out,
+            narrowing_first_moment,
+            narrowing_raw_moment,
+            layernorm_scale_bias,
+            layernorm_first_moment,
+            layernorm_raw_moment,
+        ],
+    )
+    results = list(results)
+    results[:2] = [r[0, 0] for r in results[:2]]
+    results[2:5] = [r.T for r in results[2:5]]
+    return tuple(results)
+
+
 def solution(mesh):
     in_specs = (
         P(("fsdp", "dp"), None),
@@ -443,6 +1749,7 @@
         P(None, "fsdp"),
         P(None, "fsdp"),
     )
+    own_plan = dict(mesh.shape) == {"fsdp": 16, "dp": 2}
     return jax.shard_map(
-        per_device, mesh=mesh, in_specs=in_specs, out_specs=out_specs, check_vma=False
-    )
+        per_device_links if own_plan else per_device, mesh=mesh, in_specs=in_specs, out_specs=out_specs, check_vma=False
+    )

time: 1480 us -> 432 us (0.29)
  waiting for transfers between devices: 1020 us -> 118 us
  blocking collectives: 173 us -> 0 us
  Pallas kernels: 0 us -> 161 us
  matrix products: 115 us -> 0 us
  starting transfers between devices: 5.41 us -> 79.1 us
  other arithmetic: 92.3 us -> 27.8 us
  local copies, waits for them, and re-layouts: 34.1 us -> 18.7 us
    reduce_scatter x5 -> x0, waiting for transfers between devices: 577 us -> none  [the longest x1 174 us: per_device(): lax.psum_scatter(grads[4], 'fsdp', scatter_dimension=0, tiled=True)]
    all_gather x6 -> x1, waiting for transfers between devices: 341 us -> 0.02 us  [per_device_links(): lax.all_gather(after(down_half, *near), 'fsdp', axis=0, tiled=True)]
    pallas_call x0 -> x13, Pallas kernels: none -> 161 us  [staged_call(): pl.pallas_call(kernel, out_shape=shapes, in_specs=[pl.BlockSpec(memory_sp...]
    ppermute x0 -> x79, waiting for transfers between devices: none -> 118 us  [send(): return lax.ppermute(array, AXES, pairs)]
    dot_general x23 -> x0, matrix products: 115 us -> none  [the longest x1 21 us: layer_forward(): jnp.dot(normed_low, widening_matrix_in, preferred_element_type=jnp.float32)]
    all_gather x2 -> x0, blocking collectives: 88.4 us -> none  [the longest x1 45.8 us: per_device(): lax.all_gather(kmer_identifiers.reshape(-1), 'fsdp', axis=0, tiled=True)]
    psum x3 -> x0, blocking collectives: 84.6 us -> none  [the longest x1 42.8 us: per_device(): grad_norm = jnp.sqrt(lax.psum(squares, 'fsdp'))]
    unnamed x14 -> x1, waiting for transfers between devices: 84.3 us -> 0.02 us
  transfers between devices with their start and end apart: 14 -> 80, of which waited for: 12 -> 29; matrix products, arithmetic and copies ran while one was open for 12% -> 10% of each run, Pallas kernels for 0% -> 35%
where the time goes in v1:
time: 432 us; the launch traced here: 424 us
  Pallas kernels  161 us (37%)
  waiting for transfers between devices  118 us (27%)
  starting transfers between devices  79.1 us (18%)
  other arithmetic  27.8 us (6%)
  between operations  19.9 us (5%)
  local copies, waits for them, and re-layouts  18.7 us (4%)
    pallas_call x13, Pallas kernels, staged_call(): pl.pallas_call(kernel, out_shape=shapes, in_specs=[pl.BlockSpec(memory_sp...  161 us
    ppermute x79, waiting for transfers between devices, send(): return lax.ppermute(array, AXES, pairs)  118 us
    ppermute x79, starting transfers between devices, send(): return lax.ppermute(array, AXES, pairs)  79 us
  transfers between devices with their start and end apart: 80, of which 29 were waited for; matrix products, arithmetic and copies ran while one was open for 10% of the time, Pallas kernels for 35%

profile of v1, /device:TPU:0, one launch (start us, length us, event | category | flops | bytes accessed | tf_op | source)
XLA Modules:
  0.0 423.7 jit_solution(4288117848961892283)
XLA Ops:
  38.9 6.7 %shard_map.383 = (bf16[192,512]{1,0:T(8,128)(2,1)}, bf16[192,512]{1,0:T(8,128)(2,1)}, bf16[192,512]{1,0:T(8,128)(2,1)}, bf16[192,512]{1,0:T(8,128)(2,1)}) custom-call(s32[9]{0:T(128)} %stack.490.refs_0_, s32[4,1,512]{2,1,0:T(1,128)} %pad_add_fusion.refs_1_, bf16[48,4352]{1,0:T(8,128)(2,1)} %pad.8.refs_2_, bf16[48,2176]{1,0:T(8,128)(2,1)} %copy-done.10, ...), custom_call_target="tpu_custom_call" | custom-call | flops 6000000000 | tf_op jit(solution)/shard_map/pallas_call | solution.py:541
  46.6 11.0 %collective-permute-done.11 = bf16[48,3200]{1,0:T(8,128)(2,1)S(1)} collective-permute-done((bf16[48,3200]{1,0:T(8,128)(2,1)S(1)}, bf16[48,3200]{1,0:T(8,128)(2,1)S(1)}, u32[]{:S(2)}, u32[]{:S(2)}) %collective-permute-start.11) | collective-permute-done | bytes 307232 | tf_op jit(solution)/shard_map/ppermute | solution.py:425
  60.9 8.6 %collective-permute-start.7 = (bf16[192,512]{1,0:T(8,128)(2,1)S(1)}, bf16[192,512]{1,0:T(8,128)(2,1)S(1)}, u32[]{:S(2)}, u32[]{:S(2)}) collective-permute-start(bf16[192,512]{1,0:T(8,128)(2,1)S(1)} %copy-done.47), channel_id=1, source_target_pairs={{0,8},{1,9},{2,10},{3,11},{4,12},{5,13},{6,14},{7,15},{8,0},{9,1},... | collective-permute-start | bytes 589832 | tf_op jit(solution)/shard_map/ppermute | solution.py:425
  72.0 7.6 %collective-permute-done.7.refs_4_ = bf16[192,512]{1,0:T(8,128)(2,1)S(1)} collective-permute-done((bf16[192,512]{1,0:T(8,128)(2,1)S(1)}, bf16[192,512]{1,0:T(8,128)(2,1)S(1)}, u32[]{:S(2)}, u32[]{:S(2)}) %collective-permute-start.7) | collective-permute-done | bytes 196640 | tf_op jit(solution)/shard_map/ppermute | solution.py:425
  79.6 11.8 %collective-permute-done.8.refs_5_ = bf16[192,512]{1,0:T(8,128)(2,1)S(1)} collective-permute-done((bf16[192,512]{1,0:T(8,128)(2,1)S(1)}, bf16[192,512]{1,0:T(8,128)(2,1)S(1)}, u32[]{:S(2)}, u32[]{:S(2)}) %collective-permute-start.8) | collective-permute-done | bytes 196640 | tf_op jit(solution)/shard_map/ppermute | solution.py:425
  91.8 17.2 %collective-permute-done.15.refs_10_ = bf16[4,48,1664]{2,1,0:T(8,128)(2,1)S(1)} collective-permute-done((bf16[4,48,1664]{2,1,0:T(8,128)(2,1)}, bf16[4,48,1664]{2,1,0:T(8,128)(2,1)S(1)}, u32[]{:S(2)}, u32[]{:S(2)}) %collective-permute-start.15) | collective-permute-done | bytes 639008 | tf_op jit(solution)/shard_map/ppermute | solution.py:425
  114.7 17.3 %shard_map.384 = (bf16[512,768]{1,0:T(8,128)(2,1)}, bf16[18,512,128]{2,1,0:T(8,128)(2,1)}, f32[512,128]{1,0:T(8,128)}, bf16[512,768]{1,0:T(8,128)(2,1)}, f32[512...) custom-call(s32[68]{0:T(128)} %concatenate.13.refs_0_, ...), custom_call_target="tpu_custom_call" | custom-call | flops 16999999488 | tf_op jit(solution)/shard_map/pallas_call | solution.py:541
  132.3 5.5 %collective-permute-done.23.refs_5_.refs_10_ = bf16[4,48,1536]{2,1,0:T(8,128)(2,1)} collective-permute-done((bf16[4,48,1536]{2,1,0:T(8,128)(2,1)S(1)}, bf16[4,48,1536]{2,1,0:T(8,128)(2,1)}, u32[]{:S(2)}, u32[]{:S(2)}) %collective-permute-start.23) | collective-permute-done | bytes 589856 | tf_op jit(solution)/shard_map/ppermute | solution.py:425
  143.7 17.9 %shard_map.385 = (bf16[512,3072]{1,0:T(8,128)(2,1)}, bf16[512,3072]{1,0:T(8,128)(2,1)}) custom-call(s32[64]{0:T(128)} %stack.538.refs_0_, bf16[512,768]{1,0:T(8,128)(2,1)} %get-tuple-element.148.refs_1_, bf16[4,48,1536]{2,1,0:T(8,128)(2,1)} %copy-done.6, bf16[4,48,1536]{2,1,0:T(8,128)(2,1)} %collective-permute-done.21.refs_3_.refs_8_, ...), custom_call_target="tpu_custom_call" | custom-call | flops 17999998976 | tf_op jit(solution)/shard_map/pallas_call | solution.py:541
  162.1 9.6 %shard_map.386 = (f32[512,768]{1,0:T(8,128)}, f32[512,128]{1,0:T(8,128)}, f32[32,768]{1,0:T(8,128)}, bf16[32,768]{1,0:T(8,128)(2,1)}, f32[32,128]{1,0:T(8,128)}) custom-call(s32[1]{0:T(128)} %bitcast.refs_0_, s32[1,512]{1,0:T(1,128)} %refs_1_.7, bf16[512,3072]{1,0:T(8,128)(2,1)} %get-tuple-element.170.refs_2_.refs_1_, ...), custom_call_target="tpu_custom_call" | custom-call | flops 10000000000 | tf_op jit(solution)/shard_map/pallas_call | solution.py:541
  171.7 7.9 %collective-permute-start.30 = (bf16[32,768]{1,0:T(8,128)(2,1)}, bf16[32,768]{1,0:T(8,128)(2,1)S(1)}, u32[]{:S(2)}, u32[]{:S(2)}) collective-permute-start(bf16[32,768]{1,0:T(8,128)(2,1)} %get-tuple-element.165), channel_id=1, source_target_pairs={{0,16},{1,17},{2,18},{3,19},{4,20},{5,21},{6,22},{7,23},{8,24},{9,... | collective-permute-start | bytes 147464 | tf_op jit(solution)/shard_map/ppermute | solution.py:425
  200.8 27.7 %shard_map.387 = (f32[8,128]{1,0:T(8,128)}, bf16[512,384]{1,0:T(8,128)(2,1)}, bf16[512,384]{1,0:T(8,128)(2,1)}, bf16[512,1536]{1,0:T(8,128)(2,1)}, bf16[512,1536...) custom-call(s32[34]{0:T(128)} %stack.537.refs_0_, f32[1]{0:T(128)} %bitcast.193.refs_1_, ...), custom_call_target="tpu_custom_call" | custom-call | flops 17999998976 | tf_op jit(solution)/shard_map/pallas_call | solution.py:541
  231.1 8.6 %shard_map.388 = (bf16[8,192,384]{2,1,0:T(8,128)(2,1)}, bf16[8,192,384]{2,1,0:T(8,128)(2,1)}) custom-call(s32[16]{0:T(128)} %stack.457.refs_0_, bf16[512,3072]{1,0:T(8,128)(2,1)} %get-tuple-element.170.refs_2_.refs_1_, bf16[512,3072]{1,0:T(8,128)(2,1)} %collective-permute-done.43.refs_2_, bf16[512,384]{1,0:T(8,128)(2,1)} %get-tuple-element.171.refs_3_, ...), custom_call_target="tpu_custom_call" | custom-call | flops 7000000000 | tf_op jit(solution)/shard_map/pallas_call | solution.py:541
  240.1 10.1 %shard_map.389 = (f32[512,768]{1,0:T(8,128)}, bf16[512,768]{1,0:T(8,128)(2,1)}, bf16[512,384]{1,0:T(8,128)(2,1)}, bf16[512,384]{1,0:T(8,128)(2,1)}, f32[8,768]{1,0:T(8,128)}) custom-call(s32[64]{0:T(128)} %stack.538.refs_0_, bf16[512,1536]{1,0:T(8,128)(2,1)} %get-tuple-element.174.refs_1_.refs_3_, bf16[512,1536]{1,0:T(8,128)(2,1)} %get-tuple-element.167.refs_2_, ...), custom_call_target="tpu_custom_call" | custom-call | flops 8999999488 | tf_op jit(solution)/shard_map/pallas_call | solution.py:541
  254.5 9.0 %shard_map.390 = (bf16[8,48,2048]{2,1,0:T(8,128)(2,1)}, bf16[8,48,2048]{2,1,0:T(8,128)(2,1)}) custom-call(s32[16]{0:T(128)} %stack.457.refs_0_, bf16[512,768]{1,0:T(8,128)(2,1)} %get-tuple-element.148.refs_1_, bf16[512,768]{1,0:T(8,128)(2,1)} %collective-permute-done.20.refs_2_, bf16[512,1536]{1,0:T(8,128)(2,1)} %get-tuple-element.174.refs_1_.refs_3_, ...), custom_call_target="tpu_custom_call" | custom-call | flops 8000000000 | tf_op jit(solution)/shard_map/pallas_call | solution.py:541
  267.1 14.7 %shard_map.391 = (bf16[512,1152]{1,0:T(8,128)(2,1)}, bf16[512,384]{1,0:T(8,128)(2,1)}, f32[512,768]{1,0:T(8,128)}) custom-call(s32[68]{0:T(128)} %concatenate.13.refs_0_, s32[1,512]{1,0:T(1,128)} %refs_1_.7, s32[512,1]{1,0:T(8,128)} %copy.62.refs_2_, bf16[18,512,128]{2,1,0:T(8,128)(2,1)} %get-tuple-element.185.refs_3_, ...), custom_call_target="tpu_custom_call" | custom-call | flops 16999999488 | tf_op jit(solution)/shard_map/pallas_call | solution.py:541
  282.9 7.7 %collective-permute-done.49 = bf16[8,48,2048]{2,1,0:T(8,128)(2,1)S(1)} collective-permute-done((bf16[8,48,2048]{2,1,0:T(8,128)(2,1)}, bf16[8,48,2048]{2,1,0:T(8,128)(2,1)S(1)}, u32[]{:S(2)}, u32[]{:S(2)}) %collective-permute-start.49) | collective-permute-done | bytes 1572896 | tf_op jit(solution)/shard_map/ppermute | solution.py:425
  298.5 12.6 %shard_map.392 = (bf16[512,1152]{1,0:T(8,128)(2,1)}, bf16[192,512]{1,0:T(8,128)(2,1)}, bf16[192,512]{1,0:T(8,128)(2,1)}, bf16[192,512]{1,0:T(8,128)(2,1)}, bf16[192,512]{1,0:T(8,128)(2,1)}) custom-call(s32[68]{0:T(128)} %concatenate.13.refs_0_, s32[1,512]{1,0:T(1,128)} %refs_1_.7, s32[512,1]{1,0:T(8,128)} %copy.62.refs_2_, ...), custom_call_target="tpu_custom_call" | custom-call | flops 15000000512 | tf_op jit(solution)/shard_map/pallas_call | solution.py:541
  315.5 6.9 %shard_map.393 = (bf16[8,48,1152]{2,1,0:T(8,128)(2,1)}, bf16[8,48,1152]{2,1,0:T(8,128)(2,1)}) custom-call(s32[16]{0:T(128)} %stack.457.refs_0_, bf16[512,768]{1,0:T(8,128)(2,1)} %get-tuple-element.169.refs_1_, bf16[512,768]{1,0:T(8,128)(2,1)} %copy-done.26, bf16[512,1152]{1,0:T(8,128)(2,1)} %get-tuple-element.196.refs_3_, ...), custom_call_target="tpu_custom_call" | custom-call | flops 6000000000 | tf_op jit(solution)/shard_map/pallas_call | solution.py:541
  322.5 5.7 %collective-permute-done.56 = bf16[192,512]{1,0:T(8,128)(2,1)} collective-permute-done((bf16[192,512]{1,0:T(8,128)(2,1)}, bf16[192,512]{1,0:T(8,128)(2,1)}, u32[]{:S(2)}, u32[]{:S(2)}) %collective-permute-start.56) | collective-permute-done | bytes 196640 | tf_op jit(solution)/shard_map/ppermute | solution.py:425
  343.2 9.2 %shard_map.394 = (bf16[2,48,2176]{2,1,0:T(8,128)(2,1)}, bf16[2,48,2176]{2,1,0:T(8,128)(2,1)}) custom-call(s32[5]{0:T(128)} %stack.435.refs_0_, s32[4,1,512]{2,1,0:T(1,128)} %pad_add_fusion.refs_1_, s32[4,1,512]{2,1,0:T(1,128)} %copy-done.52, bf16[4,192,512]{2,1,0:T(8,128)(2,1)} %copy-done.4, bf16[4,192,512]{2,1,0:T(8,128)(2,1)} %copy-done.27), custom_call_target="tpu_custom_call" | custom-call | flops 8000000000 | tf_op jit(solution)/shard_map/pallas_call | solution.py:541
  355.4 5.2 %collective-permute-done.59 = bf16[2,48,2176]{2,1,0:T(8,128)(2,1)S(1)} collective-permute-done((bf16[2,48,2176]{2,1,0:T(8,128)(2,1)}, bf16[2,48,2176]{2,1,0:T(8,128)(2,1)S(1)}, u32[]{:S(2)}, u32[]{:S(2)}) %collective-permute-start.59) | collective-permute-done | bytes 417824 | tf_op jit(solution)/shard_map/ppermute | solution.py:425
  378.6 5.5 %collective-permute-done.64 = bf16[48,1152]{1,0:T(8,128)(2,1)S(1)} collective-permute-done((bf16[48,1152]{1,0:T(8,128)(2,1)S(1)}, bf16[48,1152]{1,0:T(8,128)(2,1)S(1)}, u32[]{:S(2)}, u32[]{:S(2)}) %collective-permute-start.64) | collective-permute-done | bytes 110624 | tf_op jit(solution)/shard_map/ppermute | solution.py:425
  406.2 10.3 %shard_map.395 = (f32[1,1]{1,0:T(1,128)}, f32[1,1]{1,0:T(1,128)}, f32[48,4101]{1,0:T(8,128)}, f32[48,4101]{1,0:T(8,128)}, f32[48,4101]{1,0:T(8,128)}, /*index=5*...) custom-call(s32[1]{0:T(128)} %bitcast.refs_0_, ...), custom_call_target="tpu_custom_call" | custom-call | flops 8000000000 | tf_op jit(solution)/shard_map/pallas_call | solution.py:541
  (325 shorter events, 149.5 us)
Async XLA Ops:
  7.2 124.8 %all-gather.2.cloned.1.call-start = ((), (), s32[]{:S(2)}) async-start(), calls=%async_computation | async-start | bytes 2506752 | tf_op jit(solution)/shard_map/all_gather | solution.py:1510
  32.0 25.6 %collective-permute-start.11 = (bf16[48,3200]{1,0:T(8,128)(2,1)S(1)}, bf16[48,3200]{1,0:T(8,128)(2,1)S(1)}, u32[]{:S(2)}, u32[]{:S(2)}) collective-permute-start(bf16[48,3200]{1,0:T(8,128)(2,1)S(1)} %concatenate.14), channel_id=1, source_target_pairs={{0,16},{1,17},{2,18},{3,19},{4,20},{5,21},{6,22},{7,23},{8,24},{9,... | collective-permute-start | bytes 921608 | tf_op jit(solution)/shard_map/ppermute | solution.py:425
  35.0 22.6 %collective-permute-start.12 = (bf16[48,3200]{1,0:T(8,128)(2,1)S(1)}, bf16[48,3200]{1,0:T(8,128)(2,1)S(1)}, u32[]{:S(2)}, u32[]{:S(2)}) collective-permute-start(bf16[48,3200]{1,0:T(8,128)(2,1)S(1)} %concatenate.14), channel_id=1, source_target_pairs={{0,24},{1,25},{2,26},{3,27},{4,28},{5,29},{6,30},{7,31},{8,16},{9,... | collective-permute-start | bytes 921608 | tf_op jit(solution)/shard_map/ppermute | solution.py:425
  57.8 33.7 %collective-permute-start.13 = (bf16[4,48,1664]{2,1,0:T(8,128)(2,1)S(1)}, bf16[4,48,1664]{2,1,0:T(8,128)(2,1)}, u32[]{:S(2)}, u32[]{:S(2)}) collective-permute-start(bf16[4,48,1664]{2,1,0:T(8,128)(2,1)S(1)} %pad_maximum_fusion.1.refs_7_), channel_id=1, source_target_pairs={{0,2},{1,5},{2,0},{3,7},{4,6},{5,1},{6,4},{7,3},{8,10},{9,13},{10,... | collective-permute-start | bytes 1916936 | tf_op jit(solution)/shard_map/ppermute | solution.py:425
  69.5 21.9 %collective-permute-start.8 = (bf16[192,512]{1,0:T(8,128)(2,1)S(1)}, bf16[192,512]{1,0:T(8,128)(2,1)S(1)}, u32[]{:S(2)}, u32[]{:S(2)}) collective-permute-start(bf16[192,512]{1,0:T(8,128)(2,1)S(1)} %copy-done.46), channel_id=1, source_target_pairs={{0,16},{1,17},{2,18},{3,19},{4,20},{5,21},{6,22},{7,23},{8,24},{9,... | collective-permute-start | bytes 589832 | tf_op jit(solution)/shard_map/ppermute | solution.py:425
  70.6 20.9 %collective-permute-start.9 = (bf16[192,512]{1,0:T(8,128)(2,1)S(1)}, bf16[192,512]{1,0:T(8,128)(2,1)S(1)}, u32[]{:S(2)}, u32[]{:S(2)}) collective-permute-start(bf16[192,512]{1,0:T(8,128)(2,1)S(1)} %copy-done.45), channel_id=1, source_target_pairs={{0,24},{1,25},{2,26},{3,27},{4,28},{5,29},{6,30},{7,31},{8,16},{9,... | collective-permute-start | bytes 589832 | tf_op jit(solution)/shard_map/ppermute | solution.py:425
  110.1 22.1 %collective-permute-start.21 = (bf16[4,48,1536]{2,1,0:T(8,128)(2,1)S(1)}, bf16[4,48,1536]{2,1,0:T(8,128)(2,1)}, u32[]{:S(2)}, u32[]{:S(2)}) collective-permute-start(bf16[4,48,1536]{2,1,0:T(8,128)(2,1)S(1)} %pad_maximum_fusion.3.refs_2_.refs_7_), channel_id=1, source_target_pairs={{0,2},{1,5},{2,0},{3,7},{4,6},{5,1},{6,4},{7,3},{8,10},{9,13},{10,... | collective-permute-start | bytes 1769480 | tf_op jit(solution)/shard_map/ppermute | solution.py:425
  112.0 20.3 %collective-permute-start.22 = (bf16[4,48,1536]{2,1,0:T(8,128)(2,1)S(1)}, bf16[4,48,1536]{2,1,0:T(8,128)(2,1)}, u32[]{:S(2)}, u32[]{:S(2)}) collective-permute-start(bf16[4,48,1536]{2,1,0:T(8,128)(2,1)S(1)} %pad_maximum_fusion.3.refs_2_.refs_7_), channel_id=1, source_target_pairs={{0,4},{1,3},{2,6},{3,1},{4,0},{5,7},{6,2},{7,5},{8,12},{9,11},{10,... | collective-permute-start | bytes 1769480 | tf_op jit(solution)/shard_map/ppermute | solution.py:425
  112.8 25.0 %collective-permute-start.23 = (bf16[4,48,1536]{2,1,0:T(8,128)(2,1)S(1)}, bf16[4,48,1536]{2,1,0:T(8,128)(2,1)}, u32[]{:S(2)}, u32[]{:S(2)}) collective-permute-start(bf16[4,48,1536]{2,1,0:T(8,128)(2,1)S(1)} %pad_maximum_fusion.3.refs_2_.refs_7_), channel_id=1, source_target_pairs={{0,6},{1,7},{2,4},{3,5},{4,2},{5,3},{6,0},{7,1},{8,14},{9,15},{10,... | collective-permute-start | bytes 1769480 | tf_op jit(solution)/shard_map/ppermute | solution.py:425
  132.0 30.0 %collective-permute-start.28 = (bf16[3072,384]{1,0:T(8,128)(2,1)}, bf16[3072,384]{1,0:T(8,128)(2,1)}, u32[]{:S(2)}, u32[]{:S(2)}) collective-permute-start(bf16[3072,384]{1,0:T(8,128)(2,1)} %all-gather.2.cloned.1.call-done.refs_5_.refs_21_), channel_id=1, source_target_pairs={{0,1},{1,0},{2,3},{3,2},{4,5},{5,4},{6,7},{7,6},{8,9},{9,8},{10,11... | collective-permute-start | bytes 7077896 | tf_op jit(solution)/shard_map/ppermute | solution.py:425
  161.6 69.5 %collective-permute-start.43 = (bf16[512,3072]{1,0:T(8,128)(2,1)}, bf16[512,3072]{1,0:T(8,128)(2,1)}, u32[]{:S(2)}, u32[]{:S(2)}) collective-permute-start(bf16[512,3072]{1,0:T(8,128)(2,1)} %get-tuple-element.170.refs_2_.refs_1_), channel_id=1, source_target_pairs={{0,1},{1,0},{2,3},{3,2},{4,5},{5,4},{6,7},{7,6},{8,9},{9,8},{10,11... | collective-permute-start | bytes 9437192 | tf_op jit(solution)/shard_map/ppermute | solution.py:425
  199.5 29.0 %collective-permute-start.42 = (s32[4,1,512]{2,1,0:T(1,128)S(1)}, s32[4,1,512]{2,1,0:T(1,128)S(1)}, u32[]{:S(2)}, u32[]{:S(2)}) collective-permute-start(s32[4,1,512]{2,1,0:T(1,128)S(1)} %copy-done.17), channel_id=1, source_target_pairs={{0,1},{1,0},{2,3},{3,2},{4,5},{5,4},{6,7},{7,6},{8,9},{9,8},{10,11... | collective-permute-start | bytes 24584 | tf_op jit(solution)/shard_map/ppermute | solution.py:425
  199.6 30.2 %collective-permute-start.20 = (bf16[512,768]{1,0:T(8,128)(2,1)S(1)}, bf16[512,768]{1,0:T(8,128)(2,1)}, u32[]{:S(2)}, u32[]{:S(2)}) collective-permute-start(bf16[512,768]{1,0:T(8,128)(2,1)S(1)} %copy-done.25), channel_id=1, source_target_pairs={{0,1},{1,0},{2,3},{3,2},{4,5},{5,4},{6,7},{7,6},{8,9},{9,8},{10,11... | collective-permute-start | bytes 2359304 | tf_op jit(solution)/shard_map/ppermute | solution.py:425
  200.3 29.5 %collective-permute-start.41 = (bf16[512,768]{1,0:T(8,128)(2,1)S(1)}, bf16[512,768]{1,0:T(8,128)(2,1)S(1)}, u32[]{:S(2)}, u32[]{:S(2)}) collective-permute-start(bf16[512,768]{1,0:T(8,128)(2,1)S(1)} %copy-done.23), channel_id=1, source_target_pairs={{0,1},{1,0},{2,3},{3,2},{4,5},{5,4},{6,7},{7,6},{8,9},{9,8},{10,11... | collective-permute-start | bytes 2359304 | tf_op jit(solution)/shard_map/ppermute | solution.py:425
  200.7 29.1 %collective-permute-start.40 = (bf16[512,768]{1,0:T(8,128)(2,1)S(1)}, bf16[512,768]{1,0:T(8,128)(2,1)}, u32[]{:S(2)}, u32[]{:S(2)}) collective-permute-start(bf16[512,768]{1,0:T(8,128)(2,1)S(1)} %copy-done.24), channel_id=1, source_target_pairs={{0,1},{1,0},{2,3},{3,2},{4,5},{5,4},{6,7},{7,6},{8,9},{9,8},{10,11... | collective-permute-start | bytes 2359304 | tf_op jit(solution)/shard_map/ppermute | solution.py:425
  229.8 23.9 %collective-permute-start.39 = (bf16[512,1536]{1,0:T(8,128)(2,1)}, bf16[512,1536]{1,0:T(8,128)(2,1)}, u32[]{:S(2)}, u32[]{:S(2)}) collective-permute-start(bf16[512,1536]{1,0:T(8,128)(2,1)} %get-tuple-element.167.refs_2_), channel_id=1, source_target_pairs={{0,1},{1,0},{2,3},{3,2},{4,5},{5,4},{6,7},{7,6},{8,9},{9,8},{10,11... | collective-permute-start | bytes 4718600 | tf_op jit(solution)/shard_map/ppermute | solution.py:425
  239.7 25.5 %collective-permute-start.47 = (bf16[8,192,384]{2,1,0:T(8,128)(2,1)}, bf16[8,192,384]{2,1,0:T(8,128)(2,1)S(1)}, u32[]{:S(2)}, u32[]{:S(2)}) collective-permute-start(bf16[8,192,384]{2,1,0:T(8,128)(2,1)} %get-tuple-element.173), channel_id=1, source_target_pairs={{0,4},{1,3},{2,6},{3,1},{4,0},{5,7},{6,2},{7,5},{8,12},{9,11},{10,... | collective-permute-start | bytes 3538952 | tf_op jit(solution)/shard_map/ppermute | solution.py:425
  263.6 27.0 %collective-permute-start.49 = (bf16[8,48,2048]{2,1,0:T(8,128)(2,1)}, bf16[8,48,2048]{2,1,0:T(8,128)(2,1)S(1)}, u32[]{:S(2)}, u32[]{:S(2)}) collective-permute-start(bf16[8,48,2048]{2,1,0:T(8,128)(2,1)} %get-tuple-element.183), channel_id=1, source_target_pairs={{0,4},{1,3},{2,6},{3,1},{4,0},{5,7},{6,2},{7,5},{8,12},{9,11},{10,... | collective-permute-start | bytes 4718600 | tf_op jit(solution)/shard_map/ppermute | solution.py:425
  281.8 29.2 %collective-permute-start.54 = (bf16[512,1152]{1,0:T(8,128)(2,1)}, bf16[512,1152]{1,0:T(8,128)(2,1)}, u32[]{:S(2)}, u32[]{:S(2)}) collective-permute-start(bf16[512,1152]{1,0:T(8,128)(2,1)} %get-tuple-element.193), channel_id=1, source_target_pairs={{0,1},{1,0},{2,3},{3,2},{4,5},{5,4},{6,7},{7,6},{8,9},{9,8},{10,11... | collective-permute-start | bytes 3538952 | tf_op jit(solution)/shard_map/ppermute | solution.py:425
  333.4 29.9 %collective-permute-start.66 = (bf16[48,2048]{1,0:T(8,128)(2,1)}, bf16[48,2048]{1,0:T(8,128)(2,1)}, u32[]{:S(2)}, u32[]{:S(2)}) collective-permute-start(bf16[48,2048]{1,0:T(8,128)(2,1)} %get-tuple-element.254), channel_id=1, source_target_pairs={{0,8},{1,9},{2,10},{3,11},{4,12},{5,13},{6,14},{7,15},{8,0},{9,1},... | collective-permute-start | bytes 589832 | tf_op jit(solution)/shard_map/ppermute | solution.py:425
  336.4 28.0 %collective-permute-start.67 = (bf16[48,2048]{1,0:T(8,128)(2,1)}, bf16[48,2048]{1,0:T(8,128)(2,1)}, u32[]{:S(2)}, u32[]{:S(2)}) collective-permute-start(bf16[48,2048]{1,0:T(8,128)(2,1)} %get-tuple-element.253), channel_id=1, source_target_pairs={{0,16},{1,17},{2,18},{3,19},{4,20},{5,21},{6,22},{7,23},{8,24},{9,... | collective-permute-start | bytes 589832 | tf_op jit(solution)/shard_map/ppermute | solution.py:425
  336.7 27.6 %collective-permute-start.68 = (bf16[48,2048]{1,0:T(8,128)(2,1)}, bf16[48,2048]{1,0:T(8,128)(2,1)}, u32[]{:S(2)}, u32[]{:S(2)}) collective-permute-start(bf16[48,2048]{1,0:T(8,128)(2,1)} %get-tuple-element.252), channel_id=1, source_target_pairs={{0,24},{1,25},{2,26},{3,27},{4,28},{5,29},{6,30},{7,31},{8,16},{9,... | collective-permute-start | bytes 589832 | tf_op jit(solution)/shard_map/ppermute | solution.py:425
  343.2 46.0 %collective-permute-start.72 = (bf16[192,384]{1,0:T(8,128)(2,1)}, bf16[192,384]{1,0:T(8,128)(2,1)}, u32[]{:S(2)}, u32[]{:S(2)}) collective-permute-start(bf16[192,384]{1,0:T(8,128)(2,1)} %get-tuple-element.247.refs_7_), channel_id=1, source_target_pairs={{0,1},{1,0},{2,3},{3,2},{4,5},{5,4},{6,7},{7,6},{8,9},{9,8},{10,11... | collective-permute-start | bytes 442376 | tf_op jit(solution)/shard_map/ppermute | solution.py:425
  366.4 22.7 %collective-permute-start.71 = (bf16[48,2048]{1,0:T(8,128)(2,1)}, bf16[48,2048]{1,0:T(8,128)(2,1)S(1)}, u32[]{:S(2)}, u32[]{:S(2)}) collective-permute-start(bf16[48,2048]{1,0:T(8,128)(2,1)} %fusion.3.refs_6_), channel_id=1, source_target_pairs={{0,1},{1,0},{2,3},{3,2},{4,5},{5,4},{6,7},{7,6},{8,9},{9,8},{10,11... | collective-permute-start | bytes 589832 | tf_op jit(solution)/shard_map/ppermute | solution.py:425
  (111 other events, 1286.8 us)
Sparse Core Ops, SparseCore 0:
  38.2 81.0 all-gather.1

commit v2 on v1

--- a/solution.py
+++ b/solution.py
@@ -478,6 +478,17 @@
     return jnp.stack(halves + starts).astype(jnp.int32)
 
 
+def pair_index(place, rows):
+    halves, starts = [], []
+    for core in (place.core, 1 - place.core):
+        for b in (0, 1):
+            for j in range(4):
+                for a in (0, 1):
+                    halves.append(core)
+                    starts.append(place.chip(core, j, a, b) * rows)
+    return jnp.stack(halves + starts).astype(jnp.int32)
+
+
 def slot_index(place):
     chips = [
         place.chip(place.core, j, a, b) for b in (0, 1) for a in (0, 1) for j in range(4)
@@ -511,7 +522,28 @@
     ]
 
 
-def staged_call(body, scalars, arrays, pieces, shapes, scratch, cost):
+class Stage:
+    def __init__(self, copies_in, copies_out):
+        self.copies_in, self.copies_out = dict(enumerate(copies_in)), dict(enumerate(copies_out))
+        self.started = []
+
+    def __call__(self, *which):
+        for number in which or tuple(self.copies_in):
+            self.copies_in.pop(number).wait()
+
+    def put(self, *which):
+        for number in which or tuple(self.copies_out):
+            copy = self.copies_out.pop(number)
+            copy.start()
+            self.started.append(copy)
+
+    def finish(self):
+        self.put(*tuple(self.copies_out))
+        for copy in self.started:
+            copy.wait()
+
+
+def staged_call(body, scalars, arrays, pieces, shapes, scratch, cost, late=()):
     n_s, n_a, n_p, n_o = len(scalars), len(arrays), len(pieces), len(shapes)
 
     def kernel(*refs):
@@ -523,19 +555,12 @@
         near_out, refs = refs[:n_o], refs[n_o:]
         in_sems, out_sems, refs = refs[0], refs[1], refs[2:]
         copies = whole_copies(hbm, near_in, in_sems)
-        for copy in copies:
-            copy.start()
-
-        def ready():
-            for copy in copies:
-                copy.wait()
-
-        body(ready, *smem, *near_in, *far, *near_out, *refs)
-        copies_out = whole_copies(near_out, out, out_sems)
-        for copy in copies_out:
-            copy.start()
-        for copy in copies_out:
-            copy.wait()
+        for number, copy in enumerate(copies):
+            if number not in late:
+                copy.start()
+        stage = Stage(copies, whole_copies(near_out, out, out_sems))
+        body(stage, *smem, *near_in, *far, *near_out, *refs)
+        stage.finish()
 
     in_hbm = pl.BlockSpec(memory_space=pltpu.HBM)
     return pl.pallas_call(
@@ -559,6 +584,61 @@
 def one_hot(ids_row, start, count):
     spots = lax.broadcasted_iota(jnp.int32, (count, ids_row.shape[1]), 0) + start
     return jnp.where(spots == ids_row, 1.0, 0.0).astype(bf16)
+
+
+def prepare_kernel(
+    ready, core_ref, table_ref, in_ref, out_ref, up_ref, down_ref, norm_ref, ids_ref, weight_ref,
+    both_ref, cut_ref, half_ref, down_half_ref,
+):
+    core = core_ref[0]
+
+    def mine(ref, width, start=0):
+        return ref[:, pl.ds(pl.multiple_of(start + core * width, 128), width)].astype(bf16)
+
+    ready(1, 2, 3, 5, 6, 7)
+    for t in range(3):
+        both_ref[:, t * 384 : (t + 1) * 384] = mine(in_ref, 384, t * 768)
+    both_ref[:, 1152:1536] = mine(out_ref, 384)
+    rest = jnp.zeros((1, 16), f32)
+    heavy = [jnp.concatenate([w.astype(f32), rest], 1) for w in thirds(weight_ref[...])]
+    extra = jnp.concatenate([norm_ref[...]] + heavy + [jnp.zeros((121, 48), f32)], 0)
+    both_ref[:, 1536:1664] = extra.T.astype(bf16)
+    both_ref[:, 1664:3200] = mine(up_ref, 1536)
+    ids = jnp.concatenate([ids_ref[:, k * 128 : (k + 1) * 128] for k in range(4)], 0)
+    high = lax.shift_right_logical(ids, 6)
+    ids = jnp.concatenate([high, ids - high * 64], 0).astype(f32).astype(bf16)
+    both_ref[:, 3200:3328] = jnp.concatenate([ids, jnp.zeros((40, 128), bf16)], 0)
+    ready.put(0)
+    ready(0, 4)
+    vocab = table_ref.shape[1]
+    even = vocab - vocab % 128
+    cut_ref[:, :even] = table_ref[:, :even].astype(bf16)
+    last = [table_ref[:, even:], jnp.zeros((48, VOCAB_PAD - vocab), f32)]
+    cut_ref[:, even:] = jnp.concatenate(last, 1).astype(bf16)
+    half_ref[...] = cut_ref[:, pl.ds(pl.multiple_of(core * VOCAB_HALF, 128), VOCAB_HALF)]
+    down_half_ref[...] = mine(down_ref, 384)
+
+
+def prepare(core, arrays):
+    return staged_call(
+        prepare_kernel,
+        [core],
+        arrays,
+        [],
+        [
+            shaped(bf16, 48, 3328),
+            shaped(bf16, 48, VOCAB_PAD),
+            shaped(bf16, 48, VOCAB_HALF),
+            shaped(bf16, 192, 384),
+        ],
+        [],
+        3,
+    )
+
+
+def id_row(ids_ref, j):
+    rows = ids_ref[j]
+    return jnp.concatenate([rows[k : k + 1] for k in range(4)], 1)
 
 
 def lookup_kernel(ready, idx_ref, ids_ref, *refs):
@@ -589,7 +669,7 @@
         for k in range(VOCAB_PAD // 256):
             total += jnp.dot(
                 table[:, k * 256 : (k + 1) * 256],
-                one_hot(ids_ref[j], k * 256, 256),
+                one_hot(id_row(ids_ref, j), k * 256, 256),
                 preferred_element_type=f32,
             )
         outs[j][...] = total.astype(bf16)
@@ -626,7 +706,7 @@
             for j in range(4):
                 total += lax.dot_general(
                     block[j],
-                    one_hot(ids[j], start + low, count),
+                    one_hot(id_row(ids, j), start + low, count),
                     (((1,), (1,)), ((), ())),
                     preferred_element_type=f32,
                 )
@@ -658,24 +738,23 @@
 
 
 def all_sum(value):
-    one, two, three = (send(value, p) for p in ZS[1:])
-    value = (value + one) + (two + three)
-    value = value + send(value, FIRST)
-    return value + send(value, SECOND)
+    for pairs in (ZS[1:], [FIRST, SECOND, BOTH]):
+        one, two, three = (send(value, p) for p in pairs)
+        value = (value + one) + (two + three)
+    return value
 
 
 WINDOWS = (0, 64, 192, 256)
 SCALE = HD ** (-0.5)
 
 
-def piece_copies(idx_ref, base, pieces, target, rows, sems, first_sem, cut=None):
+def piece_copies(idx_ref, base, pieces, target, rows, sems, first_sem):
     copies = []
     for number in range(32):
         half = idx_ref[base + number]
         row = pl.multiple_of(idx_ref[base + 32 + number], 16)
-        source = pieces[number // 4].at[number % 4]
-        if cut is not None:
-            source = source.at[:, cut]
+        each = 32 // len(pieces)
+        source = pieces[number // each].at[number % each]
         copies.append(
             pltpu.make_async_copy(
                 source, target.at[half, pl.ds(row, rows), :], sems.at[first_sem + number]
@@ -736,6 +815,7 @@
     for copy in e_copies:
         copy.wait()
     e_ref[...] = et_ref[...].T
+    ready.put(0)
     for copy in w_copies:
         copy.wait()
     par_ref[...] = w_ref[0, :, 1536:1664].T.astype(f32)[:8]
@@ -748,6 +828,7 @@
             part = part.astype(bf16)
             for i in range(3):
                 qkv_ref[t * 6 + k * 3 + i] = part[:, i * 128 : (i + 1) * 128]
+    ready.put(1, 7, 8)
     lse_ref[...] = jnp.zeros_like(lse_ref)
     lane = lax.broadcasted_iota(jnp.int32, (128, 128), 1)
     left = lane < HD
@@ -771,6 +852,7 @@
             cols = pl.ds(pl.multiple_of(pair * 128, 128), 128)
             mixed_ref[rows, cols] = jnp.where(left, mixed[:128], mixed[128:]).astype(bf16)
 
+    ready.put(2, 3)
     for k in range(2):
         attended_ref[:, k * 384 : (k + 1) * 384] = nn_dot(mixed_ref[...], w_ref[k, :, 1152:1536])
     for b in range(4):
@@ -810,24 +892,24 @@
 
 
 def gelu_and_slope(u):
-    square = 0.5 * u * u
-    t = 1.0 / (1.0 + (0.5 * 0.5**0.5) * jnp.abs(u))
-    poly = 0.17087277
+    bell = jnp.exp(-0.5 * u * u)
+    base = 1.0 + (0.3275911 * 0.5**0.5) * jnp.abs(u)
+    t = pl.reciprocal(base, approx=True)
+    t = t * (2.0 - base * t)
+    poly = -0.07032334059476852
     for factor in (
-        -0.82215223,
-        1.48851587,
-        -1.13520398,
-        0.27886807,
-        -0.18628806,
-        0.09678418,
-        0.37409196,
-        1.00002368,
-        -1.26551223,
+        0.24725385010242462,
+        -0.2008872926235199,
+        0.2245105654001236,
+        0.013965459540486336,
+        0.10251718759536743,
+        0.09044301509857178,
+        0.09252061694860458,
     ):
         poly = factor + t * poly
-    tail = (0.5 * t) * jnp.exp(poly - square)
+    tail = (t * poly) * bell
     phi = jnp.where(u < 0, tail, 1.0 - tail)
-    return u * phi, phi + (u * 0.3989422804014327) * jnp.exp(-square)
+    return u * phi, phi + (u * 0.3989422804014327) * bell
 
 
 def up_kernel(ready, idx_ref, low_ref, *refs):
@@ -875,16 +957,9 @@
     return high, middle, (rest - middle.astype(f32)).astype(bf16)
 
 
-def half_copies(core, own, other, target, sems):
-    return [
-        pltpu.make_async_copy(own, target.at[core], sems.at[0]),
-        pltpu.make_async_copy(other, target.at[1 - core], sems.at[1]),
-    ]
-
-
 def down_kernel(ready, idx_ref, seg_row_ref, act_ref, unit_one_ref, par_ref, *refs):
-    unit_ref, inv_ref, frag_ref, frag_low_ref, size_ref, w_ref, result_ref, sems = refs[2:]
-    copies = half_copies(idx_ref[0], refs[0], refs[1], w_ref, sems)
+    unit_ref, inv_ref, frag_ref, frag_low_ref, size_ref, w_ref, result_ref, sems = refs[4:]
+    copies = piece_copies(idx_ref, 0, refs[:4], w_ref, 192, sems, 0)
     for copy in copies:
         copy.start()
     ready()
@@ -927,7 +1002,7 @@
         [
             pltpu.VMEM((2, 3072, 384), bf16),
             pltpu.VMEM((512, 768), f32),
-            pltpu.SemaphoreType.DMA((2,)),
+            pltpu.SemaphoreType.DMA((32,)),
         ],
         10,
     )
@@ -943,12 +1018,12 @@
 
 
 def loss_kernel(
-    ready, idx_ref, heat_ref, seg_col_ref, partner_ref, own_weight_ref, partner_row_ref, side_ref,
+    ready, idx_ref, heat_ref, seg_col_ref, partner_ref, own_weight_ref, side_ref,
     frag_ref, size_ref, unit_ref, inv_ref, par_ref, slope_ref, *refs
 ):
-    blocks, down_pieces = refs[:8], refs[8:10]
-    loss_ref, low_own_ref, low_other_ref, gup_own_ref, gup_other_ref, two_ref, gains_ref = refs[10:17]
-    all_ref, down_ref, low_ref, spread_ref, sems, w_sems = refs[17:]
+    blocks, down_pieces = refs[:8], refs[8:12]
+    loss_ref, low_own_ref, low_other_ref, gup_own_ref, gup_other_ref, two_ref, gains_ref = refs[12:19]
+    all_ref, down_ref, low_ref, spread_ref, sems, w_sems = refs[19:]
     copies = []
     for number in range(32):
         row = pl.multiple_of(idx_ref[1 + number], 16)
@@ -958,12 +1033,15 @@
             )
         )
     core = idx_ref[33]
-    down_copies = half_copies(core, down_pieces[0], down_pieces[1], down_ref, w_sems)
-    for copy in copies + down_copies:
+    down_copies = piece_copies(idx_ref, 34, down_pieces, down_ref, 192, w_sems, 0)
+    for copy in copies:
         copy.start()
-    ready()
     for copy in copies:
         copy.wait()
+    ready(1, 2, 3)
+    ready.copies_in[9].start()
+    for copy in down_copies:
+        copy.start()
     base = idx_ref[0]
     inv_heat = 1.0 / heat_ref[0]
     tally = 1024
@@ -973,47 +1051,42 @@
     down = lax.broadcasted_iota(jnp.int32, (32, tally), 0) + base
     powers = jnp.where(across == down, 0.0, jnp.exp(grid))
     total = jnp.sum(powers, -1, keepdims=True)
-    chosen = across == partner_ref[...]
+    eye = lax.broadcasted_iota(jnp.int32, (32, 32), 0) == lax.broadcasted_iota(jnp.int32, (32, 32), 1)
+    partner = jnp.sum(jnp.where(eye, partner_ref[...].astype(f32), 0.0), -1, keepdims=True)
+    own_weight = jnp.sum(jnp.where(eye, own_weight_ref[...], 0.0), -1, keepdims=True)
+    chosen = across == partner.astype(jnp.int32)
     target = jnp.sum(jnp.where(chosen, grid, 0.0), -1, keepdims=True)
-    terms = own_weight_ref[...] * (jnp.log(total) - target)
+    terms = own_weight * (jnp.log(total) - target)
     loss_ref[...] = jnp.broadcast_to(jnp.sum(terms, 0, keepdims=True) / tally, (8, 128))
-    pull = powers / total - jnp.where(chosen, 1.0, 0.0)
-    pull = (pull * (own_weight_ref[...] * (inv_heat / tally))).astype(bf16)
-    grad = nn_dot(pull, all_ref[...])
+    picked = jnp.where(chosen, 1.0, 0.0)
+    pull = (powers / total - picked) * (own_weight * (inv_heat / tally))
+    totals = [jnp.zeros((1, 128), f32) for _ in range(8)]
+    number = lax.broadcasted_iota(jnp.int32, (128, 128), 0)
+    same = number == lax.broadcasted_iota(jnp.int32, (128, 128), 1)
+    weights = []
     for big in range(2):
-        many = all_ref[big * 512 : (big + 1) * 512, :]
-        spread_ref[...] = nt_dot(many, all_ref[...])
-        close = nt_dot(many, mine)
-        parts = []
+        spread_ref[...] = nt_dot(all_ref[big * 512 : (big + 1) * 512, :], all_ref[...])
         for b in range(big * 4, big * 4 + 4):
             inside = slice((b - big * 4) * 128, (b - big * 4 + 1) * 128)
-            spread = jnp.exp((spread_ref[inside, :] - 1.0) * inv_heat)
-            number = lax.broadcasted_iota(jnp.int32, (128, 128), 0)
-            same = number == lax.broadcasted_iota(jnp.int32, (128, 128), 1)
-            spread_total = sum(
-                jnp.where(same, 0.0, spread[:, n * 128 : (n + 1) * 128])
-                if n == b
-                else spread[:, n * 128 : (n + 1) * 128]
-                for n in range(8)
-            )
-            spread_total = jnp.sum(spread_total, -1, keepdims=True)
-            part = jnp.exp((close[inside, :] - 1.0) * inv_heat)
-            here = lax.broadcasted_iota(jnp.int32, (128, 32), 0) + b * 128
-            column = lax.broadcasted_iota(jnp.int32, (128, 32), 1) + base
-            part = jnp.where(here == column, 0.0, part) / spread_total
-            part = part - jnp.where(here == partner_row_ref[...], 1.0, 0.0)
+            for n in range(8):
+                spread = jnp.exp((spread_ref[inside, n * 128 : (n + 1) * 128] - 1.0) * inv_heat)
+                if n == b:
+                    spread = jnp.where(same, 0.0, spread)
+                totals[n] += jnp.sum(spread, 0, keepdims=True)
             side = jnp.concatenate(
                 [
                     side_ref[n % 2, (n // 2) * 48 : (n // 2) * 48 + 32, :].astype(f32)
                     for n in range(b * 4, b * 4 + 4)
                 ],
                 0,
-            )
-            lanes = lax.broadcasted_iota(jnp.int32, (128, 128), 1)
-            wanted = jnp.logical_and(lanes >= 4, lanes < 7)
-            weight = jnp.sum(jnp.where(wanted, side, 0.0), -1, keepdims=True)
-            parts.append((part * (weight * (inv_heat / tally))).astype(bf16))
-        grad += tn_dot(jnp.concatenate(parts, 0), many)
+            ).T
+            weights.append(side[4:5] + side[5:6] + side[6:7])
+    totals, weights = jnp.concatenate(totals, 1), jnp.concatenate(weights, 1)
+    column_pull = (powers / totals - picked) * (weights * (inv_heat / tally))
+    both = jnp.concatenate([pull.astype(bf16), column_pull.astype(bf16)], 0)
+    both = nn_dot(both, all_ref[...])
+    grad = both[:32] + both[32:]
+    ready(0, 4, 5, 6, 7, 8)
     frag = frag_ref[...]
     pooled = size_ref[:, 0:1] * (grad - frag * jnp.sum(grad * frag, -1, keepdims=True))
     stacked = jnp.concatenate(thirds(pooled), 0)
@@ -1033,6 +1106,8 @@
     halves = (core, 1 - core)
     for half, ref in zip(halves, (low_own_ref, low_other_ref)):
         ref[...] = low_ref[:, pl.ds(pl.multiple_of(half * 384, 128), 384)]
+    ready.put(0, 1, 2, 5)
+    ready(9)
     for copy in down_copies:
         copy.wait()
     for half, gup_ref in zip(halves, (gup_own_ref, gup_other_ref)):
@@ -1047,6 +1122,9 @@
             )
             gup_ref[:, cols] = (g * slope_ref[:, wide].astype(f32)).astype(bf16)
 
+        if gup_ref is gup_own_ref:
+            ready.put(3)
+
     gains_ref[...] = jnp.concatenate([gain_two, shift_two, jnp.zeros((6, 768), f32)], 0)
 
 
@@ -1071,9 +1149,10 @@
             pltpu.VMEM((512, 768), bf16),
             pltpu.VMEM((512, 1024), f32),
             pltpu.SemaphoreType.DMA((32,)),
-            pltpu.SemaphoreType.DMA((2,)),
+            pltpu.SemaphoreType.DMA((32,)),
         ],
         18,
+        (9,),
     )
 
 
@@ -1190,6 +1269,7 @@
             for k in range(2)
         ).astype(bf16)
     heads_back(half, gm_ref, qkv_ref, lse_ref, bias_ref, gqkv_ref, gk_ref, gv_ref)
+    ready.put(0, 1)
     for n in range(3):
         cols = slice(n * 256, (n + 1) * 256)
         part_ref[:, cols] = resid_ref[:, cols] + nt_dot(gqkv_ref[...], w_ref[half, cols, :1152])
@@ -1238,6 +1318,7 @@
         bias_ref[b] = window_bias(seg_row_ref[...], seg_col_ref[...], b)
     core = idx_ref[4]
     heads_back(core, gm_ref, qkv_ref, lse_ref, bias_ref, gqkv_ref, gk_ref, gv_ref)
+    ready.put(0)
     for copy in copies:
         copy.wait()
     for n in range(3):
@@ -1376,7 +1457,7 @@
 
 
 def optimizer_kernel(ready, core_ref, fix_ref, totals_ref, totals_o_ref, *refs):
-    ready()
+    ready(*range(10))
     own, other = refs[:4], refs[4:8]
     params, outs = refs[8:26], refs[26:46]
     table_ref = refs[46]
@@ -1400,32 +1481,53 @@
         outs[4 + 3 * number][spot] = second
 
     every = slice(None)
-    for side, (table, into, up_out, down) in enumerate((own, other)):
-        half = core if side == 0 else 1 - core
-
-        def columns(width, start=0):
-            return pl.ds(pl.multiple_of(half * width + start, 128), width)
-
-        table_ref[:, columns(VOCAB_HALF)] = table[...]
+    halves = ((core, own), (1 - core, other))
+
+    def columns(half, width, start=0):
+        return pl.ds(pl.multiple_of(half * width + start, 128), width)
+
+    def opened(number):
+        ready(*range(10 + 3 * number, 13 + 3 * number))
+
+    def done(number):
+        ready.put(*range(2 + 3 * number, 5 + 3 * number))
+
+    opened(3)
+    for half, (_, _, up_out, _) in halves:
+        for t in range(3):
+            spot = pl.ds(pl.multiple_of(half * 1536 + t * 512, 128), 512)
+            update(3, (every, spot), up_out[:, t * 512 : (t + 1) * 512], rate_matrix, decay_rate)
+    done(3)
+    opened(4)
+    for half, (_, _, _, down) in halves:
+        for t in range(4):
+            rows = slice(t * 48, (t + 1) * 48)
+            update(4, (rows, columns(half, 384)), down[rows, :], rate_matrix, decay_rate)
+    done(4)
+    opened(1)
+    for half, (_, into, _, _) in halves:
         for t in range(3):
             update(
                 1,
-                (every, columns(384, t * 768)),
+                (every, columns(half, 384, t * 768)),
                 into[:, t * 384 : (t + 1) * 384],
                 rate_matrix,
                 decay_rate,
             )
-        update(2, (every, columns(384)), up_out[:, 1536:1920], rate_matrix, decay_rate)
-        for t in range(3):
-            spot = pl.ds(pl.multiple_of(half * 1536 + t * 512, 128), 512)
-            update(3, (every, spot), up_out[:, t * 512 : (t + 1) * 512], rate_matrix, decay_rate)
-        for t in range(4):
-            rows = slice(t * 48, (t + 1) * 48)
-            update(4, (rows, columns(384)), down[rows, :], rate_matrix, decay_rate)
+    done(1)
+    opened(0)
+    for half, (table, _, _, _) in halves:
+        table_ref[:, columns(half, VOCAB_HALF)] = table[...]
     vocab = params[0].shape[1]
     for low in range(0, vocab, 512):
         spot = slice(low, min(vocab, low + 512))
         update(0, (every, spot), table_ref[:, spot], rate_embed, decay_rate)
+    done(0)
+    opened(2)
+    for half, (_, _, up_out, _) in halves:
+        update(2, (every, columns(half, 384)), up_out[:, 1536:1920], rate_matrix, decay_rate)
+    done(2)
+    opened(5)
     norms = jnp.where(core == 0, own[2][:, 1920:].astype(f32), other[2][:, 1920:].astype(f32))
     update(5, (every, every), norms.T[:4], rate_norm, 0.0)
 
@@ -1477,51 +1579,43 @@
     place = Place()
     core = place.core
     vocab = lexicon_table.shape[0]
-    table_cut = jnp.pad(lexicon_table.T.astype(bf16), ((0, 0), (0, VOCAB_PAD - vocab)))
-    table_half = my_half(table_cut, core, VOCAB_HALF)
+    core_index = core.astype(jnp.int32).reshape(1)
+    both_cut, table_cut, table_half, down_half = prepare(
+        core_index,
+        [
+            lexicon_table.T,
+            query_key_value_maps,
+            attention_exit_map,
+            widening_matrix_in,
+            narrowing_matrix_out,
+            layernorm_scale_bias,
+            kmer_identifiers,
+            fragment_weight.reshape(1, 32),
+        ],
+    )
     near = [send(table_half, FIRST), send(table_half, SECOND)]
     near.append(send(near[0], SECOND))
-    ids_z = jnp.stack(
-        [kmer_identifiers] + [send(kmer_identifiers, ZS[j]) for j in (1, 2, 3)]
-    )
-    others = send(after(jnp.stack(near), ids_z), CORE)
-    norm_cut = layernorm_scale_bias.T.astype(bf16)
-    heavy = jnp.stack(thirds(fragment_weight), 1)
-    extra = jnp.concatenate(
-        [
-            norm_cut,
-            jnp.pad(heavy, ((0, 16), (0, 0))),
-            jnp.zeros((48, 121), bf16),
-        ],
-        1,
-    )
-    low_in = query_key_value_maps.astype(bf16)
-    low_out = attention_exit_map.astype(bf16)
-    low_up = widening_matrix_in.astype(bf16)
-    low_down = narrowing_matrix_out.astype(bf16)
-    in_out_cut = jnp.concatenate(
-        [my_half(low_in[:, k * 768 : (k + 1) * 768], core, 384) for k in range(3)]
-        + [my_half(low_out, core, 384), extra],
-        1,
-    )
-    both_cut = jnp.concatenate([in_out_cut, my_half(low_up, core, 1536)], 1)
-    both_far = z_sends(after(both_cut, table_half))
-    down_half = my_half(low_down, core, 384)
-    down_own = lax.all_gather(after(down_half, *near), "fsdp", axis=0, tiled=True)
+    both_far = z_sends(both_cut)
     slots = [place.y * 2 + place.x]
     for side in (core, 1 - core):
         slots += [place.plane_slot(side, a, b) for a, b in ((1, 0), (0, 1), (1, 1))]
     index = jnp.stack(
         [s * 48 for s in slots] + [core * VOCAB_HALF, (1 - core) * VOCAB_HALF]
     ).astype(jnp.int32)
+    down_first = send(after(down_half, near[0]), FIRST)
+    others = send(after(jnp.stack(near), down_first, *both_far), CORE)
+    id_parts = jnp.stack([p[:8, 3200:] for p in both_far]).astype(f32)
+    ids_z = (id_parts[:, :4] * 64.0 + id_parts[:, 4:]).astype(jnp.int32)
+    in_out_column = jnp.stack([p[:, :1664] for p in both_far])
+    in_out_mine = plane_sends(in_out_column, True)
     found = lookup(index, ids_z, [table_cut] + near + [others])
-    both_far = together(both_far, *found)
-    in_out_column = jnp.stack([p[:, :1664] for p in both_far])
-    up_column = jnp.stack([p[:, 1664:] for p in both_far])
+    up_column = after(jnp.stack([p[:, 1664:3200] for p in both_far]), *found)
     columns = [found[0]] + [send(found[j], ZS[j]) for j in (1, 2, 3)]
-    in_out_mine = plane_sends(in_out_column, False, columns)
-    in_out = both_cores(together(in_out_mine, in_out_mine[3]))
-    up_mine = plane_sends(after(up_column, in_out_mine[3]), True)
+    in_out = both_cores(together(in_out_mine, *columns))
+    up_column = after(up_column, in_out_mine[3])
+    up_mine = [up_column, send(up_column, FIRST), send(up_column, SECOND)]
+    down_pair = jnp.stack([down_half, after(down_first, *found)])
+    down_far = z_sends(after(down_pair, *columns))
     seg_row = slot_fragment_ids
     seg_col = slot_fragment_ids.reshape(512, 1)
     index_48 = piece_index(place, 48)
@@ -1530,12 +1624,19 @@
     embedded, qkv, lse, mixed, unit_one, inv_one, normed_low, params, side = attention_forward(
         attention_index, seg_row, seg_col, columns, in_out
     )
-    up_w = both_cores(together(up_mine, normed_low))
+    *up_mine, d_one, d_two, d_three = together(up_mine + down_far[1:], normed_low)
+    up_mine.append(send(up_mine[1], SECOND))
+    down_one = jnp.stack([down_far[0], d_one, d_two, d_three]).reshape(8, 192, 384)
+    down_two = send(down_one, SECOND)
+    down_one_o = send(down_one, CORE)
+    up_w = both_cores(up_mine)
     activated, slope = up_forward(index_48, normed_low, up_w)
-    down_w = [down_own, send(after(down_own, normed_low), CORE)]
-    core_index = core.astype(jnp.int32).reshape(1)
+    down_two, down_one_o = together([down_two, down_one_o], activated)
+    down_w = [down_one, down_two, down_one_o, send(down_two, CORE)]
+    index_192 = pair_index(place, 192)
+    base = (lax.axis_index("fsdp") * 2 + core) * 32
     unit_two, inv_two, unit_rows, unit_low, unit_scale = down_forward(
-        core_index, seg_row, activated, unit_one, params, down_w
+        index_192, seg_row, activated, unit_one, params, down_w
     )
     embedded_o, mixed_o, normed_o, activated_o = (
         send(a, CORE) for a in (embedded, mixed, normed_low, activated)
@@ -1543,7 +1644,6 @@
     column = jnp.stack([unit_low] + [send(unit_low, ZS[j]) for j in (1, 2, 3)])
     blocks = [column, send(column, FIRST), send(column, SECOND), send(column, BOTH)]
     blocks = blocks + [send(block, CORE) for block in blocks]
-    base = (lax.axis_index("fsdp") * 2 + core) * 32
     index = [base]
     for who in (core, 1 - core):
         for a, b in ((0, 0), (1, 0), (0, 1), (1, 1)):
@@ -1552,13 +1652,12 @@
     (
         loss_tile, grad_result_own, grad_result_x, grad_up_own, grad_up_x, grad_two, gains_two,
     ) = loss_backward(
-        jnp.stack(index).astype(jnp.int32),
+        jnp.concatenate([jnp.stack(index).astype(jnp.int32), index_192]),
         affinity_heat.reshape(1),
         [
             seg_col,
-            mirror_fragment_index.reshape(32, 1),
-            fragment_weight.reshape(32, 1),
             mirror_fragment_index.reshape(1, 32),
+            fragment_weight.reshape(1, 32),
             side,
             unit_rows,
             unit_scale,
@@ -1610,22 +1709,23 @@
         in_out,
     )
     grad_qkv_o = send(grad_qkv_x, CORE)
-    down_came_two, up_out_came = together([down_came_two, up_out_came], part)
+    down_came_two = after(down_came_two, part)
     down_here, down_far = scatter_here(down_keep, down_came, down_came_two)
-    up_out_across = scatter_add(up_out_keep, up_out_came)
-    up_out_came_two = send(up_out_across, FIRST)
     down_far_came = line_sends(down_far)
     grad_qkv_own, *outs = own_heads(
         attention_index,
-        [seg_row, seg_col, qkv, lse, grad_mixed_own, after(part, up_out_across, *down_far)],
+        [seg_row, seg_col, qkv, lse, grad_mixed_own, after(part, *down_far)],
         in_out[:4],
     )
     far_cols = [send(outs[j], ZS[j]) for j in (1, 2, 3)]
-    *down_far_came, up_out_came_two, grad_qkv_o = together(
-        down_far_came + [up_out_came_two, grad_qkv_o], grad_qkv_own
-    )
-    down_sum = line_sum(down_here, down_far_came)
-    in_keep, in_away = in_grad(slots, [embedded, embedded_o, grad_qkv_own, grad_qkv_o])
+    *down_far_came, up_out_came, grad_qkv_o = together(
+        down_far_came + [up_out_came, grad_qkv_o], grad_qkv_own
+    )
+    up_out_across = scatter_add(up_out_keep, up_out_came)
+    up_out_came_two = send(up_out_across, FIRST)
+    in_keep, in_away = in_grad(
+        slots, [embedded, embedded_o, after(grad_qkv_own, up_out_across), grad_qkv_o]
+    )
     far_cols = together(far_cols, in_away)
     in_came = send(after(in_away, *far_cols), SECOND)
     token_cols = jnp.stack([outs[0]] + far_cols)
@@ -1643,6 +1743,7 @@
         token_cols_o,
     )
     came = send(away, SECOND)
+    down_sum = line_sum(after(down_here, away), down_far_came)
     in_came = after(in_came, away)
     in_across = scatter_add(in_keep, in_came)
     in_came_two = send(in_across, FIRST)
@@ -1655,7 +1756,7 @@
     table_sum = table_sum.astype(bf16)
     in_sum = line_sum(in_here, together(in_far_came, table_sum))
     sums = [table_sum, in_sum, up_out_sum, down_sum]
-    sums_o = [send(s, CORE) for s in sums]
+    sums_o = [send(s, CORE) for s in together(sums, table_sum)]
     squares = sum(
         jnp.sum(jnp.square(p.astype(f32)))
         for p in (sums[0], sums[1], sums[2][:, :1920], sums[3])

time: 432 us -> 376 us (0.87)
  waiting for transfers between devices: 118 us -> 80.3 us
  between operations: 19.9 us -> 6.5 us
  starting transfers between devices: 79.1 us -> 84.5 us
  other arithmetic: 27.8 us -> 22.8 us
    ppermute x79 -> x83, waiting for transfers between devices: 118 us -> 80.3 us  [send(): return lax.ppermute(array, AXES, pairs)]
    ppermute x79 -> x83, starting transfers between devices: 79 us -> 84.5 us  [send(): return lax.ppermute(array, AXES, pairs)]
    pallas_call x13 -> x14, Pallas kernels: 161 us -> 158 us  [staged_call(): pl.pallas_call(kernel, out_shape=shapes, in_specs=[pl.BlockSpec(memory_sp...]
  transfers between devices with their start and end apart: 80 -> 83, of which waited for: 29 -> 26; matrix products, arithmetic and copies ran while one was open for 10% -> 9% of each run, Pallas kernels for 35% -> 40%
where the time goes in v2:
time: 376 us; the launch traced here: 369 us
  Pallas kernels  158 us (42%)
  starting transfers between devices  84.5 us (22%)
  waiting for transfers between devices  80.3 us (21%)
  other arithmetic  22.8 us (6%)
  local copies, waits for them, and re-layouts  17.5 us (5%)
  between operations  6.5 us (2%)
    pallas_call x14, Pallas kernels, staged_call(): pl.pallas_call(kernel, out_shape=shapes, in_specs=[pl.BlockSpec(memory_sp...  158 us
    ppermute x83, starting transfers between devices, send(): return lax.ppermute(array, AXES, pairs)  84.5 us
    ppermute x83, waiting for transfers between devices, send(): return lax.ppermute(array, AXES, pairs)  80.3 us
  transfers between devices with their start and end apart: 83, of which 26 were waited for; matrix products, arithmetic and copies ran while one was open for 9% of the time, Pallas kernels for 40%

profile of v2, /device:TPU:0, one launch (start us, length us, event | category | flops | bytes accessed | tf_op | source)
XLA Modules:
  0.0 369.0 jit_solution(2976888400508258709)
XLA Ops:
  3.4 5.1 %collective-permute-start.2 = (bf16[48,3328]{1,0:T(8,128)(2,1)}, bf16[48,3328]{1,0:T(8,128)(2,1)S(1)}, u32[]{:S(2)}, u32[]{:S(2)}) collective-permute-start(bf16[48,3328]{1,0:T(8,128)(2,1)} %get-tuple-element.142), channel_id=1, source_target_pairs={{0,24},{1,25},{2,26},{3,27},{4,28},{5,29},{6,30},{7,31},{8,16},{9,... | collective-permute-start | bytes 958472 | tf_op jit(solution)/shard_map/ppermute | solution.py:425
  19.0 17.0 %collective-permute-done.1 = bf16[48,3328]{1,0:T(8,128)(2,1)S(1)} collective-permute-done((bf16[48,3328]{1,0:T(8,128)(2,1)}, bf16[48,3328]{1,0:T(8,128)(2,1)S(1)}, u32[]{:S(2)}, u32[]{:S(2)}) %collective-permute-start.1) | collective-permute-done | bytes 319520 | tf_op jit(solution)/shard_map/ppermute | solution.py:425
  42.9 6.5 %shard_map.384 = (bf16[192,512]{1,0:T(8,128)(2,1)}, bf16[192,512]{1,0:T(8,128)(2,1)}, bf16[192,512]{1,0:T(8,128)(2,1)}, bf16[192,512]{1,0:T(8,128)(2,1)}) custom-call(s32[9]{0:T(128)} %stack.614.refs_0_, s32[4,4,128]{2,1,0:T(4,128)} %fusion.17.refs_1_, bf16[48,4352]{1,0:T(8,128)(2,1)} %get-tuple-element.143.refs_2_, bf16[48,2176]{1,0:T(8,128)(2,1)} %copy-done.9, ...), custom_call_target="tpu_custom_call" | custom-call | flops 6000000000 | tf_op jit(solution)/shard_map/pallas_call | solution.py:566
  55.9 10.7 %collective-permute-done.13.refs_10_ = bf16[4,48,1664]{2,1,0:T(8,128)(2,1)} collective-permute-done((bf16[4,48,1664]{2,1,0:T(8,128)(2,1)S(1)}, bf16[4,48,1664]{2,1,0:T(8,128)(2,1)}, u32[]{:S(2)}, u32[]{:S(2)}) %collective-permute-start.13) | collective-permute-done | bytes 639008 | tf_op jit(solution)/shard_map/ppermute | solution.py:425
  71.3 3.9 %collective-permute-start.21 = (bf16[2,192,384]{2,1,0:T(8,128)(2,1)S(1)}, bf16[2,192,384]{2,1,0:T(8,128)(2,1)S(1)}, u32[]{:S(2)}, u32[]{:S(2)}) collective-permute-start(bf16[2,192,384]{2,1,0:T(8,128)(2,1)S(1)} %pad_maximum_fusion.5), channel_id=1, source_target_pairs={{0,8},{1,9},{2,10},{3,11},{4,12},{5,13},{6,14},{7,15},{8,0},{9,1},... | collective-permute-start | bytes 884744 | tf_op jit(solution)/shard_map/ppermute | solution.py:425
  79.4 17.1 %shard_map.385 = (bf16[512,768]{1,0:T(8,128)(2,1)}, bf16[18,512,128]{2,1,0:T(8,128)(2,1)}, f32[512,128]{1,0:T(8,128)}, bf16[512,768]{1,0:T(8,128)(2,1)}, f32[512...) custom-call(s32[68]{0:T(128)} %concatenate.14.refs_0_, ...), custom_call_target="tpu_custom_call" | custom-call | flops 16999999488 | tf_op jit(solution)/shard_map/pallas_call | solution.py:566
  100.4 8.7 %collective-permute-done.24.refs_5_.refs_10_ = bf16[4,48,1536]{2,1,0:T(8,128)(2,1)} collective-permute-done((bf16[4,48,1536]{2,1,0:T(8,128)(2,1)}, bf16[4,48,1536]{2,1,0:T(8,128)(2,1)}, u32[]{:S(2)}, u32[]{:S(2)}) %collective-permute-start.24) | collective-permute-done | bytes 589856 | tf_op jit(solution)/shard_map/ppermute | solution.py:425
  111.4 16.6 %shard_map.386 = (bf16[512,3072]{1,0:T(8,128)(2,1)}, bf16[512,3072]{1,0:T(8,128)(2,1)}) custom-call(s32[64]{0:T(128)} %stack.682.refs_0_, bf16[512,768]{1,0:T(8,128)(2,1)} %get-tuple-element.156.refs_1_, bf16[4,48,1536]{2,1,0:T(8,128)(2,1)} %copy-done.7, bf16[4,48,1536]{2,1,0:T(8,128)(2,1)} %collective-permute-done.19.refs_3_.refs_8_, ...), custom_call_target="tpu_custom_call" | custom-call | flops 17999998976 | tf_op jit(solution)/shard_map/pallas_call | solution.py:566
  132.2 10.5 %shard_map.387 = (f32[512,768]{1,0:T(8,128)}, f32[512,128]{1,0:T(8,128)}, f32[32,768]{1,0:T(8,128)}, bf16[32,768]{1,0:T(8,128)(2,1)}, f32[32,128]{1,0:T(8,128)}) custom-call(s32[64]{0:T(128)} %stack.681.refs_0_, s32[1,512]{1,0:T(1,128)} %refs_1_.7, bf16[512,3072]{1,0:T(8,128)(2,1)} %get-tuple-element.183.refs_2_.refs_1_, ...), custom_call_target="tpu_custom_call" | custom-call | flops 10000000000 | tf_op jit(solution)/shard_map/pallas_call | solution.py:566
  145.2 4.6 %collective-permute-start.33 = (bf16[32,768]{1,0:T(8,128)(2,1)}, bf16[32,768]{1,0:T(8,128)(2,1)S(1)}, u32[]{:S(2)}, u32[]{:S(2)}) collective-permute-start(bf16[32,768]{1,0:T(8,128)(2,1)} %get-tuple-element.178), channel_id=1, source_target_pairs={{0,16},{1,17},{2,18},{3,19},{4,20},{5,21},{6,22},{7,23},{8,24},{9,... | collective-permute-start | bytes 147464 | tf_op jit(solution)/shard_map/ppermute | solution.py:425
  158.5 4.2 %collective-permute-done.35.refs_13_ = bf16[4,32,768]{2,1,0:T(8,128)(2,1)S(1)} collective-permute-done((bf16[4,32,768]{2,1,0:T(8,128)(2,1)S(1)}, bf16[4,32,768]{2,1,0:T(8,128)(2,1)S(1)}, u32[]{:S(2)}, u32[]{:S(2)}) %collective-permute-start.35) | collective-permute-done | bytes 196640 | tf_op jit(solution)/shard_map/ppermute | solution.py:425
  169.0 24.9 %shard_map.388 = (f32[8,128]{1,0:T(8,128)}, bf16[512,384]{1,0:T(8,128)(2,1)}, bf16[512,384]{1,0:T(8,128)(2,1)}, bf16[512,1536]{1,0:T(8,128)(2,1)}, bf16[512,1536...) custom-call(s32[98]{0:T(128)} %concatenate.15.refs_0_, f32[1]{0:T(128)} %bitcast.212.refs_1_, ...), custom_call_target="tpu_custom_call" | custom-call | flops 17999998976 | tf_op jit(solution)/shard_map/pallas_call | solution.py:566
  197.7 8.7 %shard_map.389 = (bf16[8,192,384]{2,1,0:T(8,128)(2,1)}, bf16[8,192,384]{2,1,0:T(8,128)(2,1)}) custom-call(s32[16]{0:T(128)} %stack.581.refs_0_, bf16[512,3072]{1,0:T(8,128)(2,1)} %get-tuple-element.183.refs_2_.refs_1_, bf16[512,3072]{1,0:T(8,128)(2,1)} %copy-done.20, bf16[512,384]{1,0:T(8,128)(2,1)} %get-tuple-element.184.refs_3_, bf16[512,384]{1,0:T(8,128)(2,1)} %copy-done.28), custom_call_target="tpu_custom_call" | custom-call | flops 7000000000 | tf_op jit(solution)/shard_map/pallas_call | solution.py:566
  207.8 10.1 %shard_map.390 = (f32[512,768]{1,0:T(8,128)}, bf16[512,768]{1,0:T(8,128)(2,1)}, bf16[512,384]{1,0:T(8,128)(2,1)}, bf16[512,384]{1,0:T(8,128)(2,1)}, f32[8,768]{1,0:T(8,128)}) custom-call(s32[64]{0:T(128)} %stack.682.refs_0_, bf16[512,1536]{1,0:T(8,128)(2,1)} %get-tuple-element.187.refs_1_.refs_3_, bf16[512,1536]{1,0:T(8,128)(2,1)} %get-tuple-element.180.refs_2_, ...), custom_call_target="tpu_custom_call" | custom-call | flops 8999999488 | tf_op jit(solution)/shard_map/pallas_call | solution.py:566
  221.8 9.2 %shard_map.391 = (bf16[8,48,2048]{2,1,0:T(8,128)(2,1)}, bf16[8,48,2048]{2,1,0:T(8,128)(2,1)}) custom-call(s32[16]{0:T(128)} %stack.581.refs_0_, bf16[512,768]{1,0:T(8,128)(2,1)} %get-tuple-element.156.refs_1_, bf16[512,768]{1,0:T(8,128)(2,1)} %collective-permute-done.18.refs_2_, bf16[512,1536]{1,0:T(8,128)(2,1)} %get-tuple-element.187.refs_1_.refs_3_, ...), custom_call_target="tpu_custom_call" | custom-call | flops 8000000000 | tf_op jit(solution)/shard_map/pallas_call | solution.py:566
  235.1 14.7 %shard_map.392 = (bf16[512,1152]{1,0:T(8,128)(2,1)}, bf16[512,384]{1,0:T(8,128)(2,1)}, f32[512,768]{1,0:T(8,128)}) custom-call(s32[68]{0:T(128)} %concatenate.14.refs_0_, s32[1,512]{1,0:T(1,128)} %refs_1_.7, s32[512,1]{1,0:T(8,128)} %copy.44.refs_2_, bf16[18,512,128]{2,1,0:T(8,128)(2,1)} %get-tuple-element.198.refs_3_, ...), custom_call_target="tpu_custom_call" | custom-call | flops 16999999488 | tf_op jit(solution)/shard_map/pallas_call | solution.py:566
  257.4 12.7 %shard_map.393 = (bf16[512,1152]{1,0:T(8,128)(2,1)}, bf16[192,512]{1,0:T(8,128)(2,1)}, bf16[192,512]{1,0:T(8,128)(2,1)}, bf16[192,512]{1,0:T(8,128)(2,1)}, bf16[192,512]{1,0:T(8,128)(2,1)}) custom-call(s32[68]{0:T(128)} %concatenate.14.refs_0_, s32[1,512]{1,0:T(1,128)} %refs_1_.7, s32[512,1]{1,0:T(8,128)} %copy.44.refs_2_, ...), custom_call_target="tpu_custom_call" | custom-call | flops 15000000512 | tf_op jit(solution)/shard_map/pallas_call | solution.py:566
  276.8 6.7 %shard_map.394 = (bf16[8,48,1152]{2,1,0:T(8,128)(2,1)}, bf16[8,48,1152]{2,1,0:T(8,128)(2,1)}) custom-call(s32[16]{0:T(128)} %stack.581.refs_0_, bf16[512,768]{1,0:T(8,128)(2,1)} %get-tuple-element.182.refs_1_, bf16[512,768]{1,0:T(8,128)(2,1)} %collective-permute-done.44.refs_2_, bf16[512,1152]{1,0:T(8,128)(2,1)} %get-tuple-element.214.refs_3_, ...), custom_call_target="tpu_custom_call" | custom-call | flops 6000000000 | tf_op jit(solution)/shard_map/pallas_call | solution.py:566
  283.5 4.2 %collective-permute-done.59 = bf16[192,512]{1,0:T(8,128)(2,1)} collective-permute-done((bf16[192,512]{1,0:T(8,128)(2,1)}, bf16[192,512]{1,0:T(8,128)(2,1)}, u32[]{:S(2)}, u32[]{:S(2)}) %collective-permute-start.59) | collective-permute-done | bytes 196640 | tf_op jit(solution)/shard_map/ppermute | solution.py:425
  301.4 9.0 %shard_map.395 = (bf16[2,48,2176]{2,1,0:T(8,128)(2,1)}, bf16[2,48,2176]{2,1,0:T(8,128)(2,1)}) custom-call(s32[5]{0:T(128)} %stack.559.refs_0_, s32[4,4,128]{2,1,0:T(4,128)} %fusion.17.refs_1_, s32[4,4,128]{2,1,0:T(4,128)} %copy-done.38, bf16[4,192,512]{2,1,0:T(8,128)(2,1)} %pad_maximum_fusion.1.refs_3_, bf16[4,192,512]{2,1,0:T(8,128)(2,1)} %collective-permute-done.61.refs_4_), custom_call_target="tpu_custom_call" | custom-call | flops 8000000000 | tf_op jit(solution)/shard_map/pallas_call | solution.py:566
  316.0 4.3 %collective-permute-done.62 = bf16[2,48,2176]{2,1,0:T(8,128)(2,1)S(1)} collective-permute-done((bf16[2,48,2176]{2,1,0:T(8,128)(2,1)}, bf16[2,48,2176]{2,1,0:T(8,128)(2,1)S(1)}, u32[]{:S(2)}, u32[]{:S(2)}) %collective-permute-start.62) | collective-permute-done | bytes 417824 | tf_op jit(solution)/shard_map/ppermute | solution.py:425
  331.0 6.3 %collective-permute-done.67 = bf16[48,1152]{1,0:T(8,128)(2,1)S(1)} collective-permute-done((bf16[48,1152]{1,0:T(8,128)(2,1)S(1)}, bf16[48,1152]{1,0:T(8,128)(2,1)S(1)}, u32[]{:S(2)}, u32[]{:S(2)}) %collective-permute-start.67) | collective-permute-done | bytes 110624 | tf_op jit(solution)/shard_map/ppermute | solution.py:425
  349.1 3.6 collective-permute-done.78
  360.5 8.1 %shard_map.396 = (f32[1,1]{1,0:T(1,128)}, f32[1,1]{1,0:T(1,128)}, f32[48,4101]{1,0:T(8,128)}, f32[48,4101]{1,0:T(8,128)}, f32[48,4101]{1,0:T(8,128)}, /*index=5*...) custom-call(s32[1]{0:T(128)} %bitcast.refs_0_, ...), custom_call_target="tpu_custom_call" | custom-call | flops 8000000000 | tf_op jit(solution)/shard_map/pallas_call | solution.py:566
  (289 shorter events, 135.2 us)
Async XLA Ops:
  8.5 27.4 %collective-permute-start.1 = (bf16[48,3328]{1,0:T(8,128)(2,1)}, bf16[48,3328]{1,0:T(8,128)(2,1)S(1)}, u32[]{:S(2)}, u32[]{:S(2)}) collective-permute-start(bf16[48,3328]{1,0:T(8,128)(2,1)} %get-tuple-element.142), channel_id=1, source_target_pairs={{0,16},{1,17},{2,18},{3,19},{4,20},{5,21},{6,22},{7,23},{8,24},{9,... | collective-permute-start | bytes 958472 | tf_op jit(solution)/shard_map/ppermute | solution.py:425
  8.5 27.5 %collective-permute-start = (bf16[48,3328]{1,0:T(8,128)(2,1)}, bf16[48,3328]{1,0:T(8,128)(2,1)S(1)}, u32[]{:S(2)}, u32[]{:S(2)}) collective-permute-start(bf16[48,3328]{1,0:T(8,128)(2,1)} %get-tuple-element.142), channel_id=1, source_target_pairs={{0,8},{1,9},{2,10},{3,11},{4,12},{5,13},{6,14},{7,15},{8,0},{9,1},... | collective-permute-start | bytes 958472 | tf_op jit(solution)/shard_map/ppermute | solution.py:425
  10.8 28.4 %collective-permute-start.4 = (bf16[48,2176]{1,0:T(8,128)(2,1)}, bf16[48,2176]{1,0:T(8,128)(2,1)S(1)}, u32[]{:S(2)}, u32[]{:S(2)}) collective-permute-start(bf16[48,2176]{1,0:T(8,128)(2,1)} %get-tuple-element.144), channel_id=1, source_target_pairs={{0,4},{1,3},{2,6},{3,1},{4,0},{5,7},{6,2},{7,5},{8,12},{9,11},{10,... | collective-permute-start | bytes 626696 | tf_op jit(solution)/shard_map/ppermute | solution.py:425
  17.2 22.7 %collective-permute-start.6 = (bf16[192,384]{1,0:T(8,128)(2,1)}, bf16[192,384]{1,0:T(8,128)(2,1)S(1)}, u32[]{:S(2)}, u32[]{:S(2)}) collective-permute-start(bf16[192,384]{1,0:T(8,128)(2,1)} %get-tuple-element.146), channel_id=1, source_target_pairs={{0,2},{1,5},{2,0},{3,7},{4,6},{5,1},{6,4},{7,3},{8,10},{9,13},{10,... | collective-permute-start | bytes 442376 | tf_op jit(solution)/shard_map/ppermute | solution.py:425
  18.5 21.4 %collective-permute-start.5 = (bf16[48,2176]{1,0:T(8,128)(2,1)S(1)}, bf16[48,2176]{1,0:T(8,128)(2,1)S(1)}, u32[]{:S(2)}, u32[]{:S(2)}) collective-permute-start(bf16[48,2176]{1,0:T(8,128)(2,1)S(1)} %collective-permute-done.3.refs_3_), channel_id=1, source_target_pairs={{0,4},{1,3},{2,6},{3,1},{4,0},{5,7},{6,2},{7,5},{8,12},{9,11},{10,... | collective-permute-start | bytes 626696 | tf_op jit(solution)/shard_map/ppermute | solution.py:425
  39.3 27.4 %collective-permute-start.13 = (bf16[4,48,1664]{2,1,0:T(8,128)(2,1)S(1)}, bf16[4,48,1664]{2,1,0:T(8,128)(2,1)}, u32[]{:S(2)}, u32[]{:S(2)}) collective-permute-start(bf16[4,48,1664]{2,1,0:T(8,128)(2,1)S(1)} %pad_maximum_fusion.2.refs_7_), channel_id=1, source_target_pairs={{0,6},{1,7},{2,4},{3,5},{4,2},{5,3},{6,0},{7,1},{8,14},{9,15},{10,... | collective-permute-start | bytes 1916936 | tf_op jit(solution)/shard_map/ppermute | solution.py:425
  68.1 30.6 %collective-permute-start.19 = (bf16[4,48,1536]{2,1,0:T(8,128)(2,1)S(1)}, bf16[4,48,1536]{2,1,0:T(8,128)(2,1)}, u32[]{:S(2)}, u32[]{:S(2)}) collective-permute-start(bf16[4,48,1536]{2,1,0:T(8,128)(2,1)S(1)} %pad_maximum_fusion.4.refs_2_.refs_7_), channel_id=1, source_target_pairs={{0,2},{1,5},{2,0},{3,7},{4,6},{5,1},{6,4},{7,3},{8,10},{9,13},{10,... | collective-permute-start | bytes 1769480 | tf_op jit(solution)/shard_map/ppermute | solution.py:425
  69.8 29.0 %collective-permute-start.20 = (bf16[4,48,1536]{2,1,0:T(8,128)(2,1)S(1)}, bf16[4,48,1536]{2,1,0:T(8,128)(2,1)}, u32[]{:S(2)}, u32[]{:S(2)}) collective-permute-start(bf16[4,48,1536]{2,1,0:T(8,128)(2,1)S(1)} %pad_maximum_fusion.4.refs_2_.refs_7_), channel_id=1, source_target_pairs={{0,4},{1,3},{2,6},{3,1},{4,0},{5,7},{6,2},{7,5},{8,12},{9,11},{10,... | collective-permute-start | bytes 1769480 | tf_op jit(solution)/shard_map/ppermute | solution.py:425
  71.3 25.1 %collective-permute-start.21 = (bf16[2,192,384]{2,1,0:T(8,128)(2,1)S(1)}, bf16[2,192,384]{2,1,0:T(8,128)(2,1)S(1)}, u32[]{:S(2)}, u32[]{:S(2)}) collective-permute-start(bf16[2,192,384]{2,1,0:T(8,128)(2,1)S(1)} %pad_maximum_fusion.5), channel_id=1, source_target_pairs={{0,8},{1,9},{2,10},{3,11},{4,12},{5,13},{6,14},{7,15},{8,0},{9,1},... | collective-permute-start | bytes 884744 | tf_op jit(solution)/shard_map/ppermute | solution.py:425
  75.3 23.5 %collective-permute-start.22 = (bf16[2,192,384]{2,1,0:T(8,128)(2,1)S(1)}, bf16[2,192,384]{2,1,0:T(8,128)(2,1)S(1)}, u32[]{:S(2)}, u32[]{:S(2)}) collective-permute-start(bf16[2,192,384]{2,1,0:T(8,128)(2,1)S(1)} %pad_maximum_fusion.5), channel_id=1, source_target_pairs={{0,16},{1,17},{2,18},{3,19},{4,20},{5,21},{6,22},{7,23},{8,24},{9,... | collective-permute-start | bytes 884744 | tf_op jit(solution)/shard_map/ppermute | solution.py:425
  77.2 21.6 %collective-permute-start.23 = (bf16[2,192,384]{2,1,0:T(8,128)(2,1)S(1)}, bf16[2,192,384]{2,1,0:T(8,128)(2,1)S(1)}, u32[]{:S(2)}, u32[]{:S(2)}) collective-permute-start(bf16[2,192,384]{2,1,0:T(8,128)(2,1)S(1)} %pad_maximum_fusion.5), channel_id=1, source_target_pairs={{0,24},{1,25},{2,26},{3,27},{4,28},{5,29},{6,30},{7,31},{8,16},{9,... | collective-permute-start | bytes 884744 | tf_op jit(solution)/shard_map/ppermute | solution.py:425
  129.8 66.2 %collective-permute-start.46 = (bf16[512,3072]{1,0:T(8,128)(2,1)}, bf16[512,3072]{1,0:T(8,128)(2,1)S(1)}, u32[]{:S(2)}, u32[]{:S(2)}) collective-permute-start(bf16[512,3072]{1,0:T(8,128)(2,1)} %get-tuple-element.183.refs_2_.refs_1_), channel_id=1, source_target_pairs={{0,1},{1,0},{2,3},{3,2},{4,5},{5,4},{6,7},{7,6},{8,9},{9,8},{10,11... | collective-permute-start | bytes 9437192 | tf_op jit(solution)/shard_map/ppermute | solution.py:425
  167.9 26.0 %collective-permute-start.45 = (s32[4,4,128]{2,1,0:T(4,128)S(1)}, s32[4,4,128]{2,1,0:T(4,128)S(1)}, u32[]{:S(2)}, u32[]{:S(2)}) collective-permute-start(s32[4,4,128]{2,1,0:T(4,128)S(1)} %copy-done.17), channel_id=1, source_target_pairs={{0,1},{1,0},{2,3},{3,2},{4,5},{5,4},{6,7},{7,6},{8,9},{9,8},{10,11... | collective-permute-start | bytes 24584 | tf_op jit(solution)/shard_map/ppermute | solution.py:425
  168.4 26.7 %collective-permute-start.18 = (bf16[512,768]{1,0:T(8,128)(2,1)}, bf16[512,768]{1,0:T(8,128)(2,1)}, u32[]{:S(2)}, u32[]{:S(2)}) collective-permute-start(bf16[512,768]{1,0:T(8,128)(2,1)} %get-tuple-element.156.refs_1_), channel_id=1, source_target_pairs={{0,1},{1,0},{2,3},{3,2},{4,5},{5,4},{6,7},{7,6},{8,9},{9,8},{10,11... | collective-permute-start | bytes 2359304 | tf_op jit(solution)/shard_map/ppermute | solution.py:425
  168.5 26.6 %collective-permute-start.44 = (bf16[512,768]{1,0:T(8,128)(2,1)}, bf16[512,768]{1,0:T(8,128)(2,1)}, u32[]{:S(2)}, u32[]{:S(2)}) collective-permute-start(bf16[512,768]{1,0:T(8,128)(2,1)} %get-tuple-element.182.refs_1_), channel_id=1, source_target_pairs={{0,1},{1,0},{2,3},{3,2},{4,5},{5,4},{6,7},{7,6},{8,9},{9,8},{10,11... | collective-permute-start | bytes 2359304 | tf_op jit(solution)/shard_map/ppermute | solution.py:425
  168.9 26.2 %collective-permute-start.43 = (bf16[512,768]{1,0:T(8,128)(2,1)}, bf16[512,768]{1,0:T(8,128)(2,1)}, u32[]{:S(2)}, u32[]{:S(2)}) collective-permute-start(bf16[512,768]{1,0:T(8,128)(2,1)} %get-tuple-element.181.refs_5_), channel_id=1, source_target_pairs={{0,1},{1,0},{2,3},{3,2},{4,5},{5,4},{6,7},{7,6},{8,9},{9,8},{10,11... | collective-permute-start | bytes 2359304 | tf_op jit(solution)/shard_map/ppermute | solution.py:425
  195.1 26.0 %collective-permute-start.42 = (bf16[512,1536]{1,0:T(8,128)(2,1)}, bf16[512,1536]{1,0:T(8,128)(2,1)}, u32[]{:S(2)}, u32[]{:S(2)}) collective-permute-start(bf16[512,1536]{1,0:T(8,128)(2,1)} %get-tuple-element.180.refs_2_), channel_id=1, source_target_pairs={{0,1},{1,0},{2,3},{3,2},{4,5},{5,4},{6,7},{7,6},{8,9},{9,8},{10,11... | collective-permute-start | bytes 4718600 | tf_op jit(solution)/shard_map/ppermute | solution.py:425
  206.4 25.6 %collective-permute-start.50 = (bf16[8,192,384]{2,1,0:T(8,128)(2,1)}, bf16[8,192,384]{2,1,0:T(8,128)(2,1)}, u32[]{:S(2)}, u32[]{:S(2)}) collective-permute-start(bf16[8,192,384]{2,1,0:T(8,128)(2,1)} %get-tuple-element.186), channel_id=1, source_target_pairs={{0,4},{1,3},{2,6},{3,1},{4,0},{5,7},{6,2},{7,5},{8,12},{9,11},{10,... | collective-permute-start | bytes 3538952 | tf_op jit(solution)/shard_map/ppermute | solution.py:425
  231.0 43.5 %collective-permute-start.55 = (bf16[8,48,2048]{2,1,0:T(8,128)(2,1)}, bf16[8,48,2048]{2,1,0:T(8,128)(2,1)S(1)}, u32[]{:S(2)}, u32[]{:S(2)}) collective-permute-start(bf16[8,48,2048]{2,1,0:T(8,128)(2,1)} %get-tuple-element.196), channel_id=1, source_target_pairs={{0,4},{1,3},{2,6},{3,1},{4,0},{5,7},{6,2},{7,5},{8,12},{9,11},{10,... | collective-permute-start | bytes 4718600 | tf_op jit(solution)/shard_map/ppermute | solution.py:425
  249.9 24.7 %collective-permute-start.56 = (bf16[512,1152]{1,0:T(8,128)(2,1)}, bf16[512,1152]{1,0:T(8,128)(2,1)}, u32[]{:S(2)}, u32[]{:S(2)}) collective-permute-start(bf16[512,1152]{1,0:T(8,128)(2,1)} %get-tuple-element.205), channel_id=1, source_target_pairs={{0,1},{1,0},{2,3},{3,2},{4,5},{5,4},{6,7},{7,6},{8,9},{9,8},{10,11... | collective-permute-start | bytes 3538952 | tf_op jit(solution)/shard_map/ppermute | solution.py:425
  292.9 20.8 %collective-permute-start.64 = (bf16[8,48,1152]{2,1,0:T(8,128)(2,1)}, bf16[8,48,1152]{2,1,0:T(8,128)(2,1)}, u32[]{:S(2)}, u32[]{:S(2)}) collective-permute-start(bf16[8,48,1152]{2,1,0:T(8,128)(2,1)} %get-tuple-element.225), channel_id=1, source_target_pairs={{0,4},{1,3},{2,6},{3,1},{4,0},{5,7},{6,2},{7,5},{8,12},{9,11},{10,... | collective-permute-start | bytes 2654216 | tf_op jit(solution)/shard_map/ppermute | solution.py:425
  296.3 25.5 %collective-permute-start.69 = (bf16[48,2048]{1,0:T(8,128)(2,1)}, bf16[48,2048]{1,0:T(8,128)(2,1)}, u32[]{:S(2)}, u32[]{:S(2)}) collective-permute-start(bf16[48,2048]{1,0:T(8,128)(2,1)} %get-tuple-element.272), channel_id=1, source_target_pairs={{0,8},{1,9},{2,10},{3,11},{4,12},{5,13},{6,14},{7,15},{8,0},{9,1},... | collective-permute-start | bytes 589832 | tf_op jit(solution)/shard_map/ppermute | solution.py:425
  299.0 22.8 %collective-permute-start.70 = (bf16[48,2048]{1,0:T(8,128)(2,1)S(1)}, bf16[48,2048]{1,0:T(8,128)(2,1)}, u32[]{:S(2)}, u32[]{:S(2)}) collective-permute-start(bf16[48,2048]{1,0:T(8,128)(2,1)S(1)} %get-tuple-element.271), channel_id=1, source_target_pairs={{0,16},{1,17},{2,18},{3,19},{4,20},{5,21},{6,22},{7,23},{8,24},{9,... | collective-permute-start | bytes 589832 | tf_op jit(solution)/shard_map/ppermute | solution.py:425
  299.9 21.9 %collective-permute-start.71 = (bf16[48,2048]{1,0:T(8,128)(2,1)S(1)}, bf16[48,2048]{1,0:T(8,128)(2,1)}, u32[]{:S(2)}, u32[]{:S(2)}) collective-permute-start(bf16[48,2048]{1,0:T(8,128)(2,1)S(1)} %get-tuple-element.270), channel_id=1, source_target_pairs={{0,24},{1,25},{2,26},{3,27},{4,28},{5,29},{6,30},{7,31},{8,16},{9,... | collective-permute-start | bytes 589832 | tf_op jit(solution)/shard_map/ppermute | solution.py:425
  (99 other events, 1017.8 us)
